TPU v7x, 512 devices: a whole 4x8x8 slice. The times are simulated.
512 devices in a mesh: fsdp: 16 (over x_hi, y), tp: 32 (over z, x_lo, core).
Axes of the slice: x: 4 (x_hi: 2, x_lo: 2; x = x_hi * 2 + x_lo), y: 8, z: 8, core: 2. Of those that a mesh axis runs over, the one named last changes fastest.
Arguments:
- attention_output: bfloat16 [3072, 8192], P('fsdp', 'tp'), may hold values from -6 to 6
- output_weight: bfloat16 [8192, 8192], P('tp', 'fsdp'), may hold values from -0.0625 to 0.0625
- adapter_down_maps: bfloat16 [64, 16, 8192], P('fsdp', None, 'tp'), may hold values from -0.0625 to 0.0625
- adapter_up_maps: bfloat16 [64, 16, 8192], P('fsdp', None, 'tp'), may hold values from -1.5 to 1.5
- adapter_index: int32 [16, 6], P('fsdp'), may hold values from 0 to 63
- lengths: int32 [16, 6], P('fsdp'), may hold values from 1 to 32
- cotangent: bfloat16 [3072, 8192], P('fsdp', 'tp'), may hold values from -6 to 6
Outputs:
- mixed: bfloat16 [3072, 8192], P('fsdp', 'tp')
- input_gradient: bfloat16 [3072, 8192], P('fsdp', 'tp')
- grad_down: float32 [64, 16, 8192], P('fsdp', None, 'tp')
- grad_up: float32 [64, 16, 8192], P('fsdp', None, 'tp')
All inputs are finite; a program needn't handle non-finite values.
Results may differ from a plain program's by a relative error of at most 0.015.
Values may be sent and summed in bfloat16 or wider, within the bound.
No kernel may reach another device: no remote copies, remote signals or barrier semaphores. Data moves between devices by JAX's collectives and lax.ppermute only.
A program may use at most 64 MiB of HBM per device.

v0:
```python
import jax
import jax.numpy as jnp
from jax import lax
from jax.sharding import PartitionSpec as P

adapter_scale = 2.0


def rank_sum(partial_value):
    return lax.psum(partial_value, "tp")


def body(
    attention_output,
    output_weight,
    adapter_down_maps,
    adapter_up_maps,
    adapter_index,
    lengths,
    cotangent,
):
    token_rows, feature_width = attention_output.shape
    slots = adapter_index.shape[1]
    slot_len = token_rows // slots
    tables = (
        lax.all_gather(adapter_down_maps, "fsdp", axis=0, tiled=True),
        lax.all_gather(adapter_up_maps, "fsdp", axis=0, tiled=True),
    )
    adapters = tables[0].shape[0]
    slot_index = adapter_index[0]
    selected_down = jnp.take(tables[0], slot_index, axis=0)
    selected_up = jnp.take(tables[1], slot_index, axis=0)
    slot_rows = attention_output.reshape(slots, slot_len, feature_width)
    rank_middle = rank_sum(
        jnp.einsum("ucd,utd->uct", slot_rows, selected_down, preferred_element_type=jnp.float32)
    ).astype(jnp.bfloat16)
    whole_weight = lax.all_gather(output_weight, "fsdp", axis=1, tiled=True)
    partial_value = jnp.dot(attention_output, whole_weight, preferred_element_type=jnp.float32)
    frozen_product = lax.psum_scatter(
        partial_value.astype(jnp.bfloat16).astype(jnp.float32).astype(jnp.bfloat16),
        "tp",
        scatter_dimension=1,
        tiled=True,
    ).astype(jnp.float32)
    adapter_output = jnp.einsum(
        "jae,jeq->jaq", rank_middle, selected_up, preferred_element_type=jnp.float32
    )
    mixed = (
        frozen_product + adapter_scale * adapter_output.reshape(token_rows, feature_width)
    ).astype(jnp.bfloat16)
    positions = lax.iota(jnp.int32, slot_len)
    live_mask = (positions[None, :] < lengths[0][:, None]).astype(jnp.bfloat16)
    grad_out = cotangent.reshape(slots, slot_len, feature_width) * live_mask[:, :, None]
    middle_gradient = rank_sum(
        adapter_scale
        * jnp.einsum("ucd,utd->uct", grad_out, selected_up, preferred_element_type=jnp.float32)
    ).astype(jnp.bfloat16)
    one_hot = (slot_index[:, None] == lax.iota(jnp.int32, adapters)[None, :]).astype(jnp.float32)
    slot_up_map = adapter_scale * jnp.einsum(
        "gnx,gnu->gxu", rank_middle, grad_out, preferred_element_type=jnp.float32
    )
    down_slot = jnp.einsum(
        "gnx,gnu->gxu", middle_gradient, slot_rows, preferred_element_type=jnp.float32
    )
    up_part = jnp.einsum("sa,srf->arf", one_hot, slot_up_map, precision=lax.Precision.HIGHEST)
    down_part = jnp.einsum("sa,srf->arf", one_hot, down_slot, precision=lax.Precision.HIGHEST)
    grad_full = lax.all_gather(
        grad_out.reshape(token_rows, feature_width), "tp", axis=1, tiled=True
    )
    contract = (((1,), (1,)), ((), ()))
    backward_pass = lax.dot_general(
        grad_full, whole_weight, contract, preferred_element_type=jnp.float32
    )
    adapter_backward = jnp.einsum(
        "jae,jeq->jaq", middle_gradient, selected_down, preferred_element_type=jnp.float32
    )
    input_gradient = (backward_pass + adapter_backward.reshape(token_rows, feature_width)).astype(
        jnp.bfloat16
    )
    down_wire = down_part.astype(jnp.bfloat16).astype(jnp.float32)
    up_wire = up_part.astype(jnp.bfloat16).astype(jnp.float32)
    grad_down, grad_up = (
        lax.psum_scatter(
            down_wire.astype(jnp.bfloat16), "fsdp", scatter_dimension=0, tiled=True
        ).astype(jnp.float32),
        lax.psum_scatter(
            up_wire.astype(jnp.bfloat16), "fsdp", scatter_dimension=0, tiled=True
        ).astype(jnp.float32),
    )
    return (mixed, input_gradient, grad_down, grad_up)


def solution(mesh):
    placed = (
        P("fsdp", "tp"),
        P("tp", "fsdp"),
        P("fsdp", None, "tp"),
        P("fsdp", None, "tp"),
        P("fsdp", None),
        P("fsdp", None),
        P("fsdp", "tp"),
    )
    return jax.shard_map(
        body,
        mesh=mesh,
        in_specs=placed,
        out_specs=(P("fsdp", "tp"), P("fsdp", "tp"), P("fsdp", None, "tp"), P("fsdp", None, "tp")),
        check_vma=False,
    )
```

profile of v0, /device:TPU:6, one launch (start us, length us, event | category | flops | bytes accessed | tf_op | source)
XLA Modules:
  0.0 815.1 jit_solution(6925793021828091862)
XLA Ops:
  7.3 0.7 all-gather.3.cloned.1.call-update
  8.0 0.7 compare_select_fusion
  8.7 43.3 %all_gather.14 = bf16[64,16,256]{2,1,0:T(8,128)(2,1)S(1)} all-gather(bf16[4,16,256]{2,1,0:T(8,128)(2,1)} %param.12), channel_id=1, replica_groups=mesh['fsdp'=16,'tp'=32] {'fsdp'}, dimensions={0}, use_global_device_ids=true | all-gather | bytes 557056 | tf_op jit(solution)/shard_map/all_gather | solution.py:27
  52.5 40.0 %all_gather.13 = bf16[64,16,256]{2,1,0:T(8,128)(2,1)S(1)} all-gather(bf16[4,16,256]{2,1,0:T(8,128)(2,1)} %param.11), channel_id=1, replica_groups=mesh['fsdp'=16,'tp'=32] {'fsdp'}, dimensions={0}, use_global_device_ids=true | all-gather | bytes 557056 | tf_op jit(solution)/shard_map/all_gather | solution.py:26
  92.5 0.5 gather_fusion
  93.1 0.7 compare_and_fusion
  93.8 0.7 fusion.15
  94.7 1.1 convolution_multiply_fusion.1
  95.8 107.2 %all-reduce = (bf16[6,32,16]{1,2,0:T(8,128)(2,1)S(1)}, bf16[6,32,16]{1,2,0:T(8,128)(2,1)S(1)}) all-reduce(f32[6,32,16]{1,2,0:T(8,128)S(1)} %convolution_bitcast_fusion, f32[6,32,16]{1,2,0:T(8,128)S(1)} %convolution_multiply_fusion.1), channel_id=1, replica_groups=mesh['fsdp'=16,'tp'=32] {'tp'}, use_global_device_ids=true, to_apply=%region_1.3 | all-reduce | flops 6144 | bytes 36864 | tf_op jit(solution)/shard_map/psum | solution.py:10
  203.0 1.1 fusion.3
  204.1 1.4 convolution_convert_fusion.1
  205.5 1.1 copy.14
  206.8 0.7 convolution_convert_fusion.2
  207.5 1.1 copy.13
  208.8 0.7 broadcast_multiply_fusion
  209.6 4.9 convolution_convert_fusion
  215.0 190.1 %reduce-scatter.8.cloned.1.call-done = bf16[4,16,256]{2,1,0:T(8,128)(2,1)} async-done(((bf16[64,16,256]{2,1,0:T(8,128)(2,1)}), bf16[4,16,256]{2,1,0:T(8,128)(2,1)}) %reduce-scatter.8.cloned.1.call-update) | async-done | bytes 32784 | tf_op jit(solution)/shard_map/reduce_scatter | solution.py:86
  405.1 1.4 convert_element_type.62
  406.5 204.7 %reduce-scatter.6.cloned.1.call-done = bf16[4,16,256]{2,1,0:T(8,128)(2,1)} async-done(((bf16[64,16,256]{2,1,0:T(8,128)(2,1)}), bf16[4,16,256]{2,1,0:T(8,128)(2,1)}) %reduce-scatter.6.cloned.1.call-update) | async-done | bytes 32784 | tf_op jit(solution)/shard_map/reduce_scatter | solution.py:83
  611.2 1.4 convert_element_type.60
  612.6 73.5 %all-gather.5.cloned.1.call-done = bf16[192,8192]{1,0:T(8,128)(2,1)} async-done(((bf16[192,256]{1,0:T(8,128)(2,1)}), bf16[192,8192]{1,0:T(8,128)(2,1)}) %all-gather.5.cloned.1.call-update) | async-done | bytes 3145744 | tf_op jit(solution)/shard_map/all_gather | solution.py:67
  686.0 5.3 fusion
  691.4 115.7 %reduce-scatter.4.cloned.1.call-done = bf16[192,256]{1,0:T(8,128)(2,1)} async-done(((bf16[192,8192]{1,0:T(8,128)(2,1)}), bf16[192,256]{1,0:T(8,128)(2,1)}) %reduce-scatter.4.cloned.1.call-update) | async-done | bytes 98320 | tf_op jit(solution)/shard_map/reduce_scatter | solution.py:39
  807.0 1.6 fusion.1
  (23 shorter events, 1.8 us)
Async XLA Ops:
  7.2 87.3 %copy-start = (bf16[192,256]{1,0:T(8,128)(2,1)S(1)}, bf16[192,256]{1,0:T(8,128)(2,1)}, u32[]{:S(2)}) copy-start(bf16[192,256]{1,0:T(8,128)(2,1)} %param.9) | copy-start | bytes 294916
  7.2 199.6 %copy-start.2 = (s32[1,6]{1,0:T(1,128)S(1)}, s32[1,6]{1,0:T(1,128)}, u32[]{:S(2)}) copy-start(s32[1,6]{1,0:T(1,128)} %param.13) | copy-start | bytes 76
  7.2 201.6 %copy-start.1 = (bf16[192,256]{1,0:T(8,128)(2,1)S(1)}, bf16[192,256]{1,0:T(8,128)(2,1)}, u32[]{:S(2)}) copy-start(bf16[192,256]{1,0:T(8,128)(2,1)} %param.15) | copy-start | bytes 294916
  7.2 202.4 %all-gather.3.cloned.1.call-start = ((), (), s32[]{:S(2)}) async-start(), calls=%async_computation.3 | async-start | bytes 4456448 | tf_op jit(solution)/shard_map/all_gather | solution.py:37
  7.9 397.2 %reduce-scatter.8.cloned.1.call-start = ((), (), s32[]{:S(2)}) async-start(), calls=%async_computation.7 | async-start | bytes 557056 | tf_op jit(solution)/shard_map/reduce_scatter | solution.py:86
  206.6 404.6 %reduce-scatter.6.cloned.1.call-start = ((), (), s32[]{:S(2)}) async-start(), calls=%async_computation.6 | async-start | bytes 557056 | tf_op jit(solution)/shard_map/reduce_scatter | solution.py:83
  208.6 477.4 %all-gather.5.cloned.1.call-start = ((), (), s32[]{:S(2)}) async-start(), calls=%async_computation.5 | async-start | bytes 3244032 | tf_op jit(solution)/shard_map/all_gather | solution.py:67
  209.5 597.5 %reduce-scatter.4.cloned.1.call-start = ((), (), s32[]{:S(2)}) async-start(), calls=%async_computation.4 | async-start | bytes 3244032 | tf_op jit(solution)/shard_map/reduce_scatter | solution.py:39
Sparse Core Ops, SparseCore 0:
  11.1 115.6 all-gather.2
  206.7 198.3 reduce-scatter.7
  410.2 200.9 reduce-scatter.5
  613.7 72.3 all-gather.4
  688.7 118.2 reduce-scatter.3
where the time goes:
time: 820 us; the launch traced here: 815 us
  waiting for transfers between devices  585 us (71%)
  blocking collectives  191 us (23%)
  matrix products  15.3 us (2%)
  between operations  13.9 us (2%)
    reduce_scatter x1, waiting for transfers between devices, body(): lax.psum_scatter(down_wire.astype(jnp.bfloat16), 'fsdp', scatter_dimensio...  205 us
    reduce_scatter x1, waiting for transfers between devices, body(): lax.psum_scatter(up_wire.astype(jnp.bfloat16), 'fsdp', scatter_dimension=...  190 us
    reduce_scatter x1, waiting for transfers between devices, body(): lax.psum_scatter(partial_value.astype(jnp.bfloat16).astype(jnp.float32).a...  116 us
    psum x1, blocking collectives, rank_sum(): return lax.psum(partial_value, 'tp')  107 us
    all_gather x1, waiting for transfers between devices, body(): lax.all_gather(grad_out.reshape(token_rows, feature_width), 'tp', axis=1,...  73.5 us
    all_gather x1, blocking collectives, body(): lax.all_gather(adapter_up_maps, 'fsdp', axis=0, tiled=True)  43.3 us
    all_gather x1, blocking collectives, body(): lax.all_gather(adapter_down_maps, 'fsdp', axis=0, tiled=True)  40 us
  transfers between devices with their start and end apart: 5, of which 4 were waited for; matrix products, arithmetic and copies ran while one was open for 3% of the time, Pallas kernels for 0%

commit v1 on v0

v1 whole, which is shorter than its diff:
```python
import jax
import jax.numpy as jnp
from jax import lax
from jax.experimental import pallas as pl
from jax.experimental.pallas import tpu as pltpu
from jax.sharding import PartitionSpec as P

AXES = ("fsdp", "tp")
SCALE = 2.0
SLOTS = 6
SLOT_LEN = 32
RANK = 16
RING = 8
BF16 = jnp.bfloat16
F32 = jnp.float32


def flat(xh, y, z, xl, c):
    return (xh * RING + y) * 4 * RING + z * 4 + xl * 2 + c


DEVICES = [
    (xh, y, z, xl, c)
    for xh in range(2)
    for y in range(RING)
    for z in range(RING)
    for xl in range(2)
    for c in range(2)
]


def pairs(move):
    return [(flat(*d), flat(*move(*d))) for d in DEVICES]


SWAP_CORE = pairs(lambda xh, y, z, xl, c: (xh, y, z, xl, 1 - c))
SWAP_LOW = pairs(lambda xh, y, z, xl, c: (xh, y, z, 1 - xl, c))
SWAP_HIGH = pairs(lambda xh, y, z, xl, c: (1 - xh, y, z, xl, c))
SWAP_Z = [pairs(lambda xh, y, z, xl, c, k=k: (xh, y, z ^ k, xl, c)) for k in (1, 2, 4)]


def to_blocks(a):
    def move(xh, y, z, xl, c):
        if c == 0:
            return (xh, y, z, xl ^ a, c)
        return (xh, (2 * z + xl) % RING, y, a ^ (z >> 2), c)

    return pairs(move)


def from_blocks(a):
    def move(xh, y, z, xl, c):
        if c == 1:
            return (xh, y, z, xl ^ a, c)
        return (xh, z, 4 * (xl ^ a) + (y >> 1), y & 1, c)

    return pairs(move)


TO_BLOCKS = [to_blocks(a) for a in (0, 1)]
FROM_BLOCKS = [from_blocks(a) for a in (0, 1)]


def along_y(xh, z, xl, c):
    return [flat(xh, k, z, xl, c) for k in range(RING)]


def along_z(xh, y, xl, c):
    return [flat(xh, y, k, xl, c) for k in range(RING)]


OUTER = [(xh, k, xl) for xh in range(2) for k in range(RING) for xl in range(2)]
GROUPS_Y = [along_y(*o, c) for o in OUTER for c in range(2)]
GROUPS_GATHER = [along_y(*o, 0) for o in OUTER] + [along_z(*o, 1) for o in OUTER]
GROUPS_SCATTER = [along_z(*o, 0) for o in OUTER] + [along_y(*o, 1) for o in OUTER]


def permute(value, where):
    return lax.ppermute(value, AXES, where)


def exchange(value, groups):
    return lax.all_to_all(value, AXES, 0, 0, axis_index_groups=groups, tiled=True)


def product_kernel(core_ref, rows_ref, near_ref, far_ref, out_ref):
    half = near_ref.shape[0]

    @pl.when(core_ref[0] == 0)
    def _():
        out_ref[...] = (
            jnp.dot(rows_ref[:, :half], near_ref[...], preferred_element_type=F32)
            + jnp.dot(rows_ref[:, half:], far_ref[...], preferred_element_type=F32)
        ).astype(out_ref.dtype)

    @pl.when(core_ref[0] != 0)
    def _():
        contract = (((1,), (1,)), ((), ()))
        for k, ref in enumerate((near_ref, far_ref)):
            out_ref[:, k * half : (k + 1) * half] = lax.dot_general(
                rows_ref[...], ref[...], contract, preferred_element_type=F32
            ).astype(out_ref.dtype)


def product(core, rows, near, far):
    count, width = rows.shape
    tile = count // 4
    whole = lambda i: (0, 0)
    return pl.pallas_call(
        product_kernel,
        grid=(count // tile,),
        in_specs=[
            pl.BlockSpec(memory_space=pltpu.SMEM),
            pl.BlockSpec((tile, width), lambda i: (i, 0)),
            pl.BlockSpec(near.shape, whole),
            pl.BlockSpec(far.shape, whole),
        ],
        out_specs=pl.BlockSpec((tile, width), lambda i: (i, 0)),
        out_shape=jax.ShapeDtypeStruct((count, width), BF16),
        compiler_params=pltpu.CompilerParams(vmem_limit_bytes=24 * 1024 * 1024),
        cost_estimate=pl.CostEstimate(
            flops=2 * count * width * width, bytes_accessed=4 * count * width + 2 * width * width, transcendentals=0
        ),
    )(core, rows, near, far)


def body(attention_output, output_weight, down_maps, up_maps, adapter_index, lengths, cotangent):
    fsdp, tp = lax.axis_index("fsdp"), lax.axis_index("tp")
    xh, z, xl, c = fsdp // RING, tp // 4, (tp // 2) % 2, tp % 2
    first = c == 0
    tokens, width = attention_output.shape
    half = tokens // 2
    own = down_maps.shape[0]

    slots = adapter_index[0]
    other_slots = permute(adapter_index, SWAP_HIGH)[0]
    table = jnp.stack([down_maps, up_maps])
    tables = exchange(jnp.broadcast_to(table[None], (RING,) + table.shape).reshape(RING, -1, width), GROUPS_Y)
    tables = tables.reshape(RING, 2, own, RANK, width)

    positions = lax.iota(jnp.int32, SLOT_LEN)
    live = (positions[None, :] < lengths[0][:, None]).astype(BF16)
    grad_out = (cotangent.reshape(SLOTS, SLOT_LEN, width) * live[:, :, None]).reshape(tokens, width)
    mine = jnp.where(first, attention_output, grad_out)
    theirs = permute(jnp.where(first, grad_out, attention_output), SWAP_CORE)
    pair = jnp.where(first, jnp.concatenate([mine, theirs], 1), jnp.concatenate([theirs, mine], 1))
    side = jnp.where(first, xl, z >> 2)
    top, bottom = pair[:half], pair[half:]
    got = [
        permute(jnp.where(side == 0, top, bottom), TO_BLOCKS[0]),
        permute(jnp.where(side == 0, bottom, top), TO_BLOCKS[1]),
    ]
    flip = (xh ^ xl) == 1
    rows_x = jnp.concatenate([got[0][:, :width], got[1][:, :width], got[0][:, width:], got[1][:, width:]], 1)
    rows_g = jnp.concatenate([jnp.where(flip, got[1], got[0]), jnp.where(flip, got[0], got[1])], 1)
    rows = jnp.where(first, rows_x, rows_g)
    gathered = exchange(jnp.broadcast_to(rows[None], (RING,) + rows.shape), GROUPS_GATHER)

    block = jnp.concatenate([output_weight, permute(output_weight, SWAP_LOW)], 0)
    near = jnp.concatenate([block, permute(block, SWAP_HIGH)], 1)
    far = permute(near, SWAP_CORE)

    partial_value = product(c.reshape(1), gathered.reshape(RING * half, 4 * width), near, far)
    spread = exchange(partial_value.reshape(RING, half, 4 * width), GROUPS_SCATTER)
    total = jnp.sum(spread.astype(F32), 0).astype(BF16)

    def pick(which):
        local = which % (RING * own)
        return tables[local // own, :, local % own]

    high = slots // (RING * own)
    other_high = other_slots // (RING * own)
    give = jnp.where((other_high == xh)[:, None, None, None], pick(other_slots), 0)
    take = permute(give.reshape(-1, width), SWAP_HIGH).reshape(SLOTS, 2, RANK, width)
    chosen = jnp.where((high == xh)[:, None, None, None], pick(slots), take)
    chosen_down = chosen[:, 0].reshape(SLOTS * RANK, width)
    chosen_up = chosen[:, 1].reshape(SLOTS * RANK, width)

    own_slot = (lax.iota(jnp.int32, tokens)[None, :] // SLOT_LEN) == lax.iota(jnp.int32, SLOTS)[:, None]
    contract = (((1,), (1,)), ((), ()))

    def rank_product(maps, values):
        every = lax.dot_general(maps, values, contract, preferred_element_type=F32)
        every = every.reshape(SLOTS, RANK, tokens)
        return jnp.sum(jnp.where(own_slot[:, None, :], every, 0.0), 0)

    sums = jnp.concatenate(
        [rank_product(chosen_down, attention_output), SCALE * rank_product(chosen_up, grad_out)], 0
    )
    for where in (SWAP_CORE, SWAP_LOW, *SWAP_Z):
        sums = sums + permute(sums, where)
    ranks = sums.astype(BF16)

    def per_slot(value):
        spread_out = jnp.where(own_slot[:, None, :], value[None], jnp.zeros((), BF16))
        return spread_out.reshape(SLOTS * RANK, tokens)

    middle, grad_middle = per_slot(ranks[:RANK]), per_slot(ranks[RANK:])

    up_terms = (SCALE * jnp.dot(middle, grad_out, preferred_element_type=F32)).astype(BF16)
    down_terms = jnp.dot(grad_middle, attention_output, preferred_element_type=F32).astype(BF16)
    terms = jnp.stack([down_terms, up_terms]).reshape(2, SLOTS, RANK * width)
    away = permute(terms.reshape(2 * SLOTS * RANK, width), SWAP_HIGH).reshape(terms.shape)
    adapters = lax.iota(jnp.int32, RING * own) + xh * (RING * own)
    hot = jnp.concatenate(
        [(adapters[:, None] == slots[None, :]), (adapters[:, None] == other_slots[None, :])], 1
    ).astype(BF16)
    both = jnp.concatenate([terms, away], 1)
    owned = jnp.einsum("as,ksw->akw", hot, both, preferred_element_type=F32).astype(BF16)
    owned = owned.reshape(RING, own * 2 * RANK, width)
    grads = jnp.sum(exchange(owned, GROUPS_Y).astype(F32), 0).reshape(own, 2, RANK, width)

    quarters = total.reshape(half, 2, 2, width)
    halves = total.reshape(half, 2, 2 * width)
    out = []
    for a in (0, 1):
        forward = jnp.where(flip, halves[:, 1 - a], halves[:, a])
        backward = quarters[:, :, a].reshape(half, 2 * width)
        out.append(permute(jnp.where(first, forward, backward), FROM_BLOCKS[a]))
    back = jnp.where(first, z >> 2, xl)
    both_halves = jnp.concatenate(
        [jnp.where(back == 0, out[0], out[1]), jnp.where(back == 0, out[1], out[0])], 0
    )
    kept = both_halves[:, :width]
    swapped = permute(both_halves[:, width:], SWAP_CORE)
    base = jnp.where(first, kept, swapped).astype(F32)
    frozen_gradient = jnp.where(first, swapped, kept).astype(F32)

    tokens_first = (((0,), (0,)), ((), ()))
    mixed = base + SCALE * lax.dot_general(middle, chosen_up, tokens_first, preferred_element_type=F32)
    input_gradient = frozen_gradient + lax.dot_general(
        grad_middle, chosen_down, tokens_first, preferred_element_type=F32
    )
    return mixed.astype(BF16), input_gradient.astype(BF16), grads[:, 0], grads[:, 1]


def solution(mesh):
    maps = P("fsdp", None, "tp")
    flat_spec = P("fsdp", "tp")
    return jax.shard_map(
        body,
        mesh=mesh,
        in_specs=(flat_spec, P("tp", "fsdp"), maps, maps, P("fsdp", None), P("fsdp", None), flat_spec),
        out_specs=(flat_spec, flat_spec, maps, maps),
        check_vma=False,
    )
```

time: 820 us -> 179 us (0.22)
  the two profiles are of different devices: /device:TPU:6 before, /device:TPU:57 now
where the time goes in v1:
time: 179 us; the launch traced here: 178 us
  starting transfers between devices  106 us (59%)
  waiting for transfers between devices  51.2 us (29%)
  local copies, waits for them, and re-layouts  7.88 us (4%)
  Pallas kernels  5.45 us (3%)
  other arithmetic  3.66 us (2%)
  matrix products  2.84 us (2%)
    ppermute x17, starting transfers between devices, permute(): return lax.ppermute(value, AXES, where)  81.4 us
    ppermute x17, waiting for transfers between devices, permute(): return lax.ppermute(value, AXES, where)  48.7 us
    all_to_all x4, starting transfers between devices, exchange(): lax.all_to_all(value, AXES, 0, 0, axis_index_groups=groups, tiled=True)  24.6 us
    pallas_call x1, Pallas kernels, product(): pl.pallas_call(product_kernel, grid=(count // tile,), in_specs=[pl.BlockS...  5.45 us
  transfers between devices with their start and end apart: 21, of which 13 were waited for; matrix products, arithmetic and copies ran while one was open for 5% of the time, Pallas kernels for 3%

profile of v1, /device:TPU:57, one launch (start us, length us, event | category | flops | bytes accessed | tf_op | source)
XLA Modules:
  0.0 178.2 jit_solution(11837664508714303759)
XLA Ops:
  2.5 2.6 %collective-permute-start = (bf16[192,256]{1,0:T(8,128)(2,1)S(1)}, bf16[192,256]{1,0:T(8,128)(2,1)S(1)}, u32[]{:S(2)}, u32[]{:S(2)}) collective-permute-start(bf16[192,256]{1,0:T(8,128)(2,1)S(1)} %get-tuple-element.9), channel_id=1, source_target_pairs={{0,1},{1,0},{2,3},{3,2},{4,5},{5,4},{6,7},{7,6},{8,9},{9,8},{10,11... | collective-permute-start | bytes 294920 | tf_op jit(solution)/shard_map/ppermute | solution.py:79
  6.7 8.3 %all-to-all-start.2 = ((bf16[8,128,256]{2,1,0:T(8,128)(2,1)}), bf16[8,128,256]{2,1,0:T(8,128)(2,1)S(1)}, u32[]{:S(2)}, u32[]{:S(2)}) async-start(bf16[8,128,256]{2,1,0:T(8,128)(2,1)} %broadcast_in_dim.109), calls=%async_computation.2 | async-start | bytes 1048576 | tf_op jit(solution)/shard_map/all_to_all | solution.py:83
  15.1 8.4 %collective-permute-start.1 = (bf16[96,512]{1,0:T(8,128)(2,1)S(1)}, bf16[96,512]{1,0:T(8,128)(2,1)S(1)}, u32[]{:S(2)}, u32[]{:S(2)}) collective-permute-start(bf16[96,512]{1,0:T(8,128)(2,1)S(1)} %get-tuple-element.16), channel_id=1, source_target_pairs={{0,0},{1,1},{2,2},{3,33},{4,4},{5,65},{6,6},{7,97},{8,8},{9,129},{... | collective-permute-start | bytes 294920 | tf_op jit(solution)/shard_map/ppermute | solution.py:79
  23.6 2.8 %collective-permute-start.2 = (bf16[96,512]{1,0:T(8,128)(2,1)S(1)}, bf16[96,512]{1,0:T(8,128)(2,1)S(1)}, u32[]{:S(2)}, u32[]{:S(2)}) collective-permute-start(bf16[96,512]{1,0:T(8,128)(2,1)S(1)} %get-tuple-element.17), channel_id=1, source_target_pairs={{0,2},{1,3},{2,0},{3,35},{4,6},{5,67},{6,4},{7,99},{8,10},{9,131},... | collective-permute-start | bytes 294920 | tf_op jit(solution)/shard_map/ppermute | solution.py:79
  26.4 3.2 %collective-permute-done.1 = bf16[96,512]{1,0:T(8,128)(2,1)S(1)} collective-permute-done((bf16[96,512]{1,0:T(8,128)(2,1)S(1)}, bf16[96,512]{1,0:T(8,128)(2,1)S(1)}, u32[]{:S(2)}, u32[]{:S(2)}) %collective-permute-start.1) | collective-permute-done | bytes 98336 | tf_op jit(solution)/shard_map/ppermute | solution.py:79
  29.6 13.6 %collective-permute-done.2 = bf16[96,512]{1,0:T(8,128)(2,1)S(1)} collective-permute-done((bf16[96,512]{1,0:T(8,128)(2,1)S(1)}, bf16[96,512]{1,0:T(8,128)(2,1)S(1)}, u32[]{:S(2)}, u32[]{:S(2)}) %collective-permute-start.2) | collective-permute-done | bytes 98336 | tf_op jit(solution)/shard_map/ppermute | solution.py:79
  44.7 3.7 %all-to-all-start = ((bf16[8,96,1024]{2,1,0:T(8,128)(2,1)}), bf16[8,96,1024]{2,1,0:T(8,128)(2,1)S(1)}, u32[]{:S(2)}, u32[]{:S(2)}) async-start(bf16[8,96,1024]{2,1,0:T(8,128)(2,1)} %broadcast_in_dim.105), calls=%async_computation | async-start | bytes 3145728 | tf_op jit(solution)/shard_map/all_to_all | solution.py:83
  50.4 8.2 %collective-permute-done.3 = bf16[256,512]{1,0:T(8,128)(2,1)S(1)} collective-permute-done((bf16[256,512]{1,0:T(8,128)(2,1)S(1)}, bf16[256,512]{1,0:T(8,128)(2,1)S(1)}, u32[]{:S(2)}, u32[]{:S(2)}) %collective-permute-start.3) | collective-permute-done | bytes 262176 | tf_op jit(solution)/shard_map/ppermute | solution.py:79
  58.6 4.3 %collective-permute-start.4 = (bf16[512,512]{1,0:T(8,128)(2,1)S(1)}, bf16[512,512]{1,0:T(8,128)(2,1)S(1)}, u32[]{:S(2)}, u32[]{:S(2)}) collective-permute-start(bf16[512,512]{1,0:T(8,128)(2,1)S(1)} %constant_dynamic-update-slice_fusion), channel_id=1, source_target_pairs={{0,256},{1,257},{2,258},{3,259},{4,260},{5,261},{6,262},{7,263},{8... | collective-permute-start | bytes 1572872 | tf_op jit(solution)/shard_map/ppermute | solution.py:79
  65.5 4.6 %collective-permute-done.4 = bf16[512,512]{1,0:T(8,128)(2,1)S(1)} collective-permute-done((bf16[512,512]{1,0:T(8,128)(2,1)S(1)}, bf16[512,512]{1,0:T(8,128)(2,1)S(1)}, u32[]{:S(2)}, u32[]{:S(2)}) %collective-permute-start.4) | collective-permute-done | bytes 524320 | tf_op jit(solution)/shard_map/ppermute | solution.py:79
  73.1 4.3 %collective-permute-start.10 = (bf16[192,256]{1,0:T(8,128)(2,1)S(1)}, bf16[192,256]{1,0:T(8,128)(2,1)S(1)}, u32[]{:S(2)}, u32[]{:S(2)}) collective-permute-start(bf16[192,256]{1,0:T(8,128)(2,1)S(1)} %bitcast_select_fusion), channel_id=1, source_target_pairs={{0,256},{1,257},{2,258},{3,259},{4,260},{5,261},{6,262},{7,263},{8... | collective-permute-start | bytes 294920 | tf_op jit(solution)/shard_map/ppermute | solution.py:79
  78.0 5.5 %shard_map.102 = bf16[768,1024]{1,0:T(8,128)(2,1)} custom-call(s32[1]{0:T(128)} %bitcast.core_ref, bf16[768,1024]{1,0:T(8,128)(2,1)S(1)} %bitcast.69, bf16[512,1024]{1,0:T(8,128)(2,1)S(1)} %pad_maximum_fusion.near_ref, bf16[512,1024]{1,0:T(8,128)(2,1)} %collective-permute-done.5.far_ref), custom_call_target="tpu_custom_call" | custom-call | flops 1610612736 | bytes 5242880 | tf_op jit(solution)/shard_map/pallas_call | solution.py:109
  83.4 6.0 %all-to-all-start.1 = ((bf16[8,96,1024]{2,1,0:T(8,128)(2,1)}), bf16[8,96,1024]{2,1,0:T(8,128)(2,1)S(1)}, u32[]{:S(2)}, u32[]{:S(2)}) async-start(bf16[8,96,1024]{2,1,0:T(8,128)(2,1)} %bitcast.3), calls=%async_computation.1 | async-start | bytes 3145728 | tf_op jit(solution)/shard_map/all_to_all | solution.py:83
  90.1 6.4 %collective-permute-start.11 = (f32[32,192]{1,0:T(8,128)S(1)}, f32[32,192]{1,0:T(8,128)S(1)}, u32[]{:S(2)}, u32[]{:S(2)}) collective-permute-start(f32[32,192]{1,0:T(8,128)S(1)} %pad_maximum_fusion.4), channel_id=1, source_target_pairs={{0,1},{1,0},{2,3},{3,2},{4,5},{5,4},{6,7},{7,6},{8,9},{9,8},{10,11... | collective-permute-start | bytes 73736 | tf_op jit(solution)/shard_map/ppermute | solution.py:79
  99.6 2.6 %collective-permute-done.12 = f32[32,192]{1,0:T(8,128)S(1)} collective-permute-done((f32[32,192]{1,0:T(8,128)S(1)}, f32[32,192]{1,0:T(8,128)S(1)}, u32[]{:S(2)}, u32[]{:S(2)}) %collective-permute-start.12) | collective-permute-done | bytes 24608 | tf_op jit(solution)/shard_map/ppermute | solution.py:79
  102.2 3.5 %collective-permute-start.13 = (f32[32,192]{1,0:T(8,128)S(1)}, f32[32,192]{1,0:T(8,128)S(1)}, u32[]{:S(2)}, u32[]{:S(2)}) collective-permute-start(f32[32,192]{1,0:T(8,128)S(1)} %add.178), channel_id=1, source_target_pairs={{0,4},{1,5},{2,6},{3,7},{4,0},{5,1},{6,2},{7,3},{8,12},{9,13},{10,... | collective-permute-start | bytes 73736 | tf_op jit(solution)/shard_map/ppermute | solution.py:79
  105.8 4.9 %collective-permute-done.13 = f32[32,192]{1,0:T(8,128)S(1)} collective-permute-done((f32[32,192]{1,0:T(8,128)S(1)}, f32[32,192]{1,0:T(8,128)S(1)}, u32[]{:S(2)}, u32[]{:S(2)}) %collective-permute-start.13) | collective-permute-done | bytes 24608 | tf_op jit(solution)/shard_map/ppermute | solution.py:79
  110.7 5.0 %collective-permute-start.14 = (f32[32,192]{1,0:T(8,128)S(1)}, f32[32,192]{1,0:T(8,128)S(1)}, u32[]{:S(2)}, u32[]{:S(2)}) collective-permute-start(f32[32,192]{1,0:T(8,128)S(1)} %add.179), channel_id=1, source_target_pairs={{0,8},{1,9},{2,10},{3,11},{4,12},{5,13},{6,14},{7,15},{8,0},{9,1},... | collective-permute-start | bytes 73736 | tf_op jit(solution)/shard_map/ppermute | solution.py:79
  115.7 2.8 %collective-permute-done.14 = f32[32,192]{1,0:T(8,128)S(1)} collective-permute-done((f32[32,192]{1,0:T(8,128)S(1)}, f32[32,192]{1,0:T(8,128)S(1)}, u32[]{:S(2)}, u32[]{:S(2)}) %collective-permute-start.14) | collective-permute-done | bytes 24608 | tf_op jit(solution)/shard_map/ppermute | solution.py:79
  118.4 6.0 %collective-permute-start.15 = (f32[32,192]{1,0:T(8,128)S(1)}, f32[32,192]{1,0:T(8,128)S(1)}, u32[]{:S(2)}, u32[]{:S(2)}) collective-permute-start(f32[32,192]{1,0:T(8,128)S(1)} %add.180), channel_id=1, source_target_pairs={{0,16},{1,17},{2,18},{3,19},{4,20},{5,21},{6,22},{7,23},{8,24},{9,... | collective-permute-start | bytes 73736 | tf_op jit(solution)/shard_map/ppermute | solution.py:79
  124.5 2.5 %collective-permute-done.15 = f32[32,192]{1,0:T(8,128)S(1)} collective-permute-done((f32[32,192]{1,0:T(8,128)S(1)}, f32[32,192]{1,0:T(8,128)S(1)}, u32[]{:S(2)}, u32[]{:S(2)}) %collective-permute-start.15) | collective-permute-done | bytes 24608 | tf_op jit(solution)/shard_map/ppermute | solution.py:79
  129.8 4.5 %collective-permute-done.16 = bf16[192,256]{1,0:T(8,128)(2,1)S(1)} collective-permute-done((bf16[192,256]{1,0:T(8,128)(2,1)S(1)}, bf16[192,256]{1,0:T(8,128)(2,1)S(1)}, u32[]{:S(2)}, u32[]{:S(2)}) %collective-permute-start.16) | collective-permute-done | bytes 98336 | tf_op jit(solution)/shard_map/ppermute | solution.py:79
  136.5 6.5 %all-to-all-start.3 = ((bf16[8,128,256]{2,1,0:T(8,128)(2,1)}), bf16[8,128,256]{2,1,0:T(8,128)(2,1)S(1)}, u32[]{:S(2)}, u32[]{:S(2)}) async-start(bf16[8,128,256]{2,1,0:T(8,128)(2,1)} %reshape.574), calls=%async_computation.3 | async-start | bytes 1048576 | tf_op jit(solution)/shard_map/all_to_all | solution.py:83
  151.3 24.2 %collective-permute-start.8 = (bf16[192,256]{1,0:T(8,128)(2,1)S(1)}, bf16[192,256]{1,0:T(8,128)(2,1)S(1)}, u32[]{:S(2)}, u32[]{:S(2)}) collective-permute-start(bf16[192,256]{1,0:T(8,128)(2,1)S(1)} %pad_maximum_fusion.1), channel_id=1, source_target_pairs={{0,1},{1,0},{2,3},{3,2},{4,5},{5,4},{6,7},{7,6},{8,9},{9,8},{10,11... | collective-permute-start | bytes 294920 | tf_op jit(solution)/shard_map/ppermute | solution.py:79
  (91 shorter events, 32.5 us)
Async XLA Ops:
  2.5 12.5 %collective-permute-start = (bf16[192,256]{1,0:T(8,128)(2,1)S(1)}, bf16[192,256]{1,0:T(8,128)(2,1)S(1)}, u32[]{:S(2)}, u32[]{:S(2)}) collective-permute-start(bf16[192,256]{1,0:T(8,128)(2,1)S(1)} %get-tuple-element.9), channel_id=1, source_target_pairs={{0,1},{1,0},{2,3},{3,2},{4,5},{5,4},{6,7},{7,6},{8,9},{9,8},{10,11... | collective-permute-start | bytes 294920 | tf_op jit(solution)/shard_map/ppermute | solution.py:79
  6.7 36.6 %all-to-all-start.2 = ((bf16[8,128,256]{2,1,0:T(8,128)(2,1)}), bf16[8,128,256]{2,1,0:T(8,128)(2,1)S(1)}, u32[]{:S(2)}, u32[]{:S(2)}) async-start(bf16[8,128,256]{2,1,0:T(8,128)(2,1)} %broadcast_in_dim.109), calls=%async_computation.2 | async-start | bytes 1048576 | tf_op jit(solution)/shard_map/all_to_all | solution.py:83
  15.1 14.5 %collective-permute-start.1 = (bf16[96,512]{1,0:T(8,128)(2,1)S(1)}, bf16[96,512]{1,0:T(8,128)(2,1)S(1)}, u32[]{:S(2)}, u32[]{:S(2)}) collective-permute-start(bf16[96,512]{1,0:T(8,128)(2,1)S(1)} %get-tuple-element.16), channel_id=1, source_target_pairs={{0,0},{1,1},{2,2},{3,33},{4,4},{5,65},{6,6},{7,97},{8,8},{9,129},{... | collective-permute-start | bytes 294920 | tf_op jit(solution)/shard_map/ppermute | solution.py:79
  23.6 19.7 %collective-permute-start.2 = (bf16[96,512]{1,0:T(8,128)(2,1)S(1)}, bf16[96,512]{1,0:T(8,128)(2,1)S(1)}, u32[]{:S(2)}, u32[]{:S(2)}) collective-permute-start(bf16[96,512]{1,0:T(8,128)(2,1)S(1)} %get-tuple-element.17), channel_id=1, source_target_pairs={{0,2},{1,3},{2,0},{3,35},{4,6},{5,67},{6,4},{7,99},{8,10},{9,131},... | collective-permute-start | bytes 294920 | tf_op jit(solution)/shard_map/ppermute | solution.py:79
  44.7 18.2 %copy-start.3 = (s32[1,6]{1,0:T(1,128)S(1)}, s32[1,6]{1,0:T(1,128)}, u32[]{:S(2)}) copy-start(s32[1,6]{1,0:T(1,128)} %param.11) | copy-start | bytes 76
  44.7 33.3 %all-to-all-start = ((bf16[8,96,1024]{2,1,0:T(8,128)(2,1)}), bf16[8,96,1024]{2,1,0:T(8,128)(2,1)S(1)}, u32[]{:S(2)}, u32[]{:S(2)}) async-start(bf16[8,96,1024]{2,1,0:T(8,128)(2,1)} %broadcast_in_dim.105), calls=%async_computation | async-start | bytes 3145728 | tf_op jit(solution)/shard_map/all_to_all | solution.py:83
  48.5 10.1 %collective-permute-start.3 = (bf16[256,512]{1,0:T(8,128)(2,1)S(1)}, bf16[256,512]{1,0:T(8,128)(2,1)S(1)}, u32[]{:S(2)}, u32[]{:S(2)}) collective-permute-start(bf16[256,512]{1,0:T(8,128)(2,1)S(1)} %copy-done.1), channel_id=1, source_target_pairs={{0,2},{1,3},{2,0},{3,1},{4,6},{5,7},{6,4},{7,5},{8,10},{9,11},{10,... | collective-permute-start | bytes 786440 | tf_op jit(solution)/shard_map/ppermute | solution.py:79
  58.6 11.4 %collective-permute-start.4 = (bf16[512,512]{1,0:T(8,128)(2,1)S(1)}, bf16[512,512]{1,0:T(8,128)(2,1)S(1)}, u32[]{:S(2)}, u32[]{:S(2)}) collective-permute-start(bf16[512,512]{1,0:T(8,128)(2,1)S(1)} %constant_dynamic-update-slice_fusion), channel_id=1, source_target_pairs={{0,256},{1,257},{2,258},{3,259},{4,260},{5,261},{6,262},{7,263},{8... | collective-permute-start | bytes 1572872 | tf_op jit(solution)/shard_map/ppermute | solution.py:79
  63.0 9.2 %collective-permute-start.9 = (s32[1,6]{1,0:T(1,128)S(1)}, s32[1,6]{1,0:T(1,128)S(1)}, u32[]{:S(2)}, u32[]{:S(2)}) collective-permute-start(s32[1,6]{1,0:T(1,128)S(1)} %copy-done.3), channel_id=1, source_target_pairs={{0,256},{1,257},{2,258},{3,259},{4,260},{5,261},{6,262},{7,263},{8... | collective-permute-start | bytes 80 | tf_op jit(solution)/shard_map/ppermute | solution.py:79
  70.2 7.8 %collective-permute-start.5 = (bf16[512,1024]{1,0:T(8,128)(2,1)S(1)}, bf16[512,1024]{1,0:T(8,128)(2,1)}, u32[]{:S(2)}, u32[]{:S(2)}) collective-permute-start(bf16[512,1024]{1,0:T(8,128)(2,1)S(1)} %pad_maximum_fusion.near_ref), channel_id=1, source_target_pairs={{0,1},{1,0},{2,3},{3,2},{4,5},{5,4},{6,7},{7,6},{8,9},{9,8},{10,11... | collective-permute-start | bytes 3145736 | tf_op jit(solution)/shard_map/ppermute | solution.py:79
  73.1 16.4 %collective-permute-start.10 = (bf16[192,256]{1,0:T(8,128)(2,1)S(1)}, bf16[192,256]{1,0:T(8,128)(2,1)S(1)}, u32[]{:S(2)}, u32[]{:S(2)}) collective-permute-start(bf16[192,256]{1,0:T(8,128)(2,1)S(1)} %bitcast_select_fusion), channel_id=1, source_target_pairs={{0,256},{1,257},{2,258},{3,259},{4,260},{5,261},{6,262},{7,263},{8... | collective-permute-start | bytes 294920 | tf_op jit(solution)/shard_map/ppermute | solution.py:79
  83.4 6.1 %copy-start = (bf16[192,256]{1,0:T(8,128)(2,1)S(1)}, bf16[192,256]{1,0:T(8,128)(2,1)}, u32[]{:S(2)}) copy-start(bf16[192,256]{1,0:T(8,128)(2,1)} %param.7) | copy-start | bytes 294916
  83.4 6.3 %copy-start.2 = (bf16[192,256]{1,0:T(8,128)(2,1)S(1)}, bf16[192,256]{1,0:T(8,128)(2,1)}, u32[]{:S(2)}) copy-start(bf16[192,256]{1,0:T(8,128)(2,1)} %param.13) | copy-start | bytes 294916
  83.4 53.0 %all-to-all-start.1 = ((bf16[8,96,1024]{2,1,0:T(8,128)(2,1)}), bf16[8,96,1024]{2,1,0:T(8,128)(2,1)S(1)}, u32[]{:S(2)}, u32[]{:S(2)}) async-start(bf16[8,96,1024]{2,1,0:T(8,128)(2,1)} %bitcast.3), calls=%async_computation.1 | async-start | bytes 3145728 | tf_op jit(solution)/shard_map/all_to_all | solution.py:83
  90.1 7.2 %collective-permute-start.11 = (f32[32,192]{1,0:T(8,128)S(1)}, f32[32,192]{1,0:T(8,128)S(1)}, u32[]{:S(2)}, u32[]{:S(2)}) collective-permute-start(f32[32,192]{1,0:T(8,128)S(1)} %pad_maximum_fusion.4), channel_id=1, source_target_pairs={{0,1},{1,0},{2,3},{3,2},{4,5},{5,4},{6,7},{7,6},{8,9},{9,8},{10,11... | collective-permute-start | bytes 73736 | tf_op jit(solution)/shard_map/ppermute | solution.py:79
  97.3 4.9 %collective-permute-start.12 = (f32[32,192]{1,0:T(8,128)S(1)}, f32[32,192]{1,0:T(8,128)S(1)}, u32[]{:S(2)}, u32[]{:S(2)}) collective-permute-start(f32[32,192]{1,0:T(8,128)S(1)} %fusion.38), channel_id=1, source_target_pairs={{0,2},{1,3},{2,0},{3,1},{4,6},{5,7},{6,4},{7,5},{8,10},{9,11},{10,... | collective-permute-start | bytes 73736 | tf_op jit(solution)/shard_map/ppermute | solution.py:79
  102.2 8.4 %collective-permute-start.13 = (f32[32,192]{1,0:T(8,128)S(1)}, f32[32,192]{1,0:T(8,128)S(1)}, u32[]{:S(2)}, u32[]{:S(2)}) collective-permute-start(f32[32,192]{1,0:T(8,128)S(1)} %add.178), channel_id=1, source_target_pairs={{0,4},{1,5},{2,6},{3,7},{4,0},{5,1},{6,2},{7,3},{8,12},{9,13},{10,... | collective-permute-start | bytes 73736 | tf_op jit(solution)/shard_map/ppermute | solution.py:79
  110.7 7.8 %collective-permute-start.14 = (f32[32,192]{1,0:T(8,128)S(1)}, f32[32,192]{1,0:T(8,128)S(1)}, u32[]{:S(2)}, u32[]{:S(2)}) collective-permute-start(f32[32,192]{1,0:T(8,128)S(1)} %add.179), channel_id=1, source_target_pairs={{0,8},{1,9},{2,10},{3,11},{4,12},{5,13},{6,14},{7,15},{8,0},{9,1},... | collective-permute-start | bytes 73736 | tf_op jit(solution)/shard_map/ppermute | solution.py:79
  118.4 8.6 %collective-permute-start.15 = (f32[32,192]{1,0:T(8,128)S(1)}, f32[32,192]{1,0:T(8,128)S(1)}, u32[]{:S(2)}, u32[]{:S(2)}) collective-permute-start(f32[32,192]{1,0:T(8,128)S(1)} %add.180), channel_id=1, source_target_pairs={{0,16},{1,17},{2,18},{3,19},{4,20},{5,21},{6,22},{7,23},{8,24},{9,... | collective-permute-start | bytes 73736 | tf_op jit(solution)/shard_map/ppermute | solution.py:79
  127.4 6.9 %collective-permute-start.16 = (bf16[192,256]{1,0:T(8,128)(2,1)S(1)}, bf16[192,256]{1,0:T(8,128)(2,1)S(1)}, u32[]{:S(2)}, u32[]{:S(2)}) collective-permute-start(bf16[192,256]{1,0:T(8,128)(2,1)S(1)} %bitcast.82), channel_id=1, source_target_pairs={{0,256},{1,257},{2,258},{3,259},{4,260},{5,261},{6,262},{7,263},{8... | collective-permute-start | bytes 294920 | tf_op jit(solution)/shard_map/ppermute | solution.py:79
  136.5 14.1 %all-to-all-start.3 = ((bf16[8,128,256]{2,1,0:T(8,128)(2,1)}), bf16[8,128,256]{2,1,0:T(8,128)(2,1)S(1)}, u32[]{:S(2)}, u32[]{:S(2)}) async-start(bf16[8,128,256]{2,1,0:T(8,128)(2,1)} %reshape.574), calls=%async_computation.3 | async-start | bytes 1048576 | tf_op jit(solution)/shard_map/all_to_all | solution.py:83
  145.0 5.7 %collective-permute-start.6 = (bf16[96,512]{1,0:T(8,128)(2,1)S(1)}, bf16[96,512]{1,0:T(8,128)(2,1)S(1)}, u32[]{:S(2)}, u32[]{:S(2)}) collective-permute-start(bf16[96,512]{1,0:T(8,128)(2,1)S(1)} %get-tuple-element.6), channel_id=1, source_target_pairs={{0,0},{1,1},{2,16},{3,3},{4,32},{5,5},{6,48},{7,7},{8,64},{9,9},{1... | collective-permute-start | bytes 294920 | tf_op jit(solution)/shard_map/ppermute | solution.py:79
  145.6 5.7 %collective-permute-start.7 = (bf16[96,512]{1,0:T(8,128)(2,1)S(1)}, bf16[96,512]{1,0:T(8,128)(2,1)S(1)}, u32[]{:S(2)}, u32[]{:S(2)}) collective-permute-start(bf16[96,512]{1,0:T(8,128)(2,1)S(1)} %get-tuple-element.7), channel_id=1, source_target_pairs={{0,16},{1,3},{2,0},{3,1},{4,48},{5,7},{6,32},{7,5},{8,80},{9,11},{... | collective-permute-start | bytes 294920 | tf_op jit(solution)/shard_map/ppermute | solution.py:79
  151.3 25.1 %collective-permute-start.8 = (bf16[192,256]{1,0:T(8,128)(2,1)S(1)}, bf16[192,256]{1,0:T(8,128)(2,1)S(1)}, u32[]{:S(2)}, u32[]{:S(2)}) collective-permute-start(bf16[192,256]{1,0:T(8,128)(2,1)S(1)} %pad_maximum_fusion.1), channel_id=1, source_target_pairs={{0,1},{1,0},{2,3},{3,2},{4,5},{5,4},{6,7},{7,6},{8,9},{9,8},{10,11... | collective-permute-start | bytes 294920 | tf_op jit(solution)/shard_map/ppermute | solution.py:79
  (1 other events, 3.7 us)

commit v2 on v1

--- a/solution.py
+++ b/solution.py
@@ -36,7 +36,6 @@
 SWAP_CORE = pairs(lambda xh, y, z, xl, c: (xh, y, z, xl, 1 - c))
 SWAP_LOW = pairs(lambda xh, y, z, xl, c: (xh, y, z, 1 - xl, c))
 SWAP_HIGH = pairs(lambda xh, y, z, xl, c: (1 - xh, y, z, xl, c))
-SWAP_Z = [pairs(lambda xh, y, z, xl, c, k=k: (xh, y, z ^ k, xl, c)) for k in (1, 2, 4)]
 
 
 def to_blocks(a):
@@ -52,7 +51,7 @@
     def move(xh, y, z, xl, c):
         if c == 1:
             return (xh, y, z, xl ^ a, c)
-        return (xh, z, 4 * (xl ^ a) + (y >> 1), y & 1, c)
+        return (xh, (z - y) % RING, 4 * (xl ^ a) + (y >> 1), y & 1, c)
 
     return pairs(move)
 
@@ -65,14 +64,15 @@
     return [flat(xh, k, z, xl, c) for k in range(RING)]
 
 
-def along_z(xh, y, xl, c):
-    return [flat(xh, y, k, xl, c) for k in range(RING)]
+def along_z(xh, y, xl, c, turn=0):
+    return [flat(xh, y, (k + turn) % RING, xl, c) for k in range(RING)]
 
 
 OUTER = [(xh, k, xl) for xh in range(2) for k in range(RING) for xl in range(2)]
 GROUPS_Y = [along_y(*o, c) for o in OUTER for c in range(2)]
+GROUPS_Z = [along_z(*o, c) for o in OUTER for c in range(2)]
 GROUPS_GATHER = [along_y(*o, 0) for o in OUTER] + [along_z(*o, 1) for o in OUTER]
-GROUPS_SCATTER = [along_z(*o, 0) for o in OUTER] + [along_y(*o, 1) for o in OUTER]
+GROUPS_SCATTER = [along_z(*o, 0, o[1]) for o in OUTER] + [along_y(*o, 1) for o in OUTER]
 
 
 def permute(value, where):
@@ -81,6 +81,10 @@
 
 def exchange(value, groups):
     return lax.all_to_all(value, AXES, 0, 0, axis_index_groups=groups, tiled=True)
+
+
+def after(value, *others):
+    return lax.optimization_barrier((value, *others))[0]
 
 
 def product_kernel(core_ref, rows_ref, near_ref, far_ref, out_ref):
@@ -133,7 +137,6 @@
     own = down_maps.shape[0]
 
     slots = adapter_index[0]
-    other_slots = permute(adapter_index, SWAP_HIGH)[0]
     table = jnp.stack([down_maps, up_maps])
     tables = exchange(jnp.broadcast_to(table[None], (RING,) + table.shape).reshape(RING, -1, width), GROUPS_Y)
     tables = tables.reshape(RING, 2, own, RANK, width)
@@ -144,6 +147,8 @@
     mine = jnp.where(first, attention_output, grad_out)
     theirs = permute(jnp.where(first, grad_out, attention_output), SWAP_CORE)
     pair = jnp.where(first, jnp.concatenate([mine, theirs], 1), jnp.concatenate([theirs, mine], 1))
+    other_slots = permute(after(adapter_index, pair), SWAP_HIGH)[0]
+    near_rows = permute(after(output_weight, pair), SWAP_LOW)
     side = jnp.where(first, xl, z >> 2)
     top, bottom = pair[:half], pair[half:]
     got = [
@@ -154,16 +159,11 @@
     rows_x = jnp.concatenate([got[0][:, :width], got[1][:, :width], got[0][:, width:], got[1][:, width:]], 1)
     rows_g = jnp.concatenate([jnp.where(flip, got[1], got[0]), jnp.where(flip, got[0], got[1])], 1)
     rows = jnp.where(first, rows_x, rows_g)
+    rows = after(rows, near_rows, tables, other_slots)
     gathered = exchange(jnp.broadcast_to(rows[None], (RING,) + rows.shape), GROUPS_GATHER)
 
-    block = jnp.concatenate([output_weight, permute(output_weight, SWAP_LOW)], 0)
+    block = jnp.concatenate([output_weight, near_rows], 0)
     near = jnp.concatenate([block, permute(block, SWAP_HIGH)], 1)
-    far = permute(near, SWAP_CORE)
-
-    partial_value = product(c.reshape(1), gathered.reshape(RING * half, 4 * width), near, far)
-    spread = exchange(partial_value.reshape(RING, half, 4 * width), GROUPS_SCATTER)
-    total = jnp.sum(spread.astype(F32), 0).astype(BF16)
-
     def pick(which):
         local = which % (RING * own)
         return tables[local // own, :, local % own]
@@ -187,9 +187,17 @@
     sums = jnp.concatenate(
         [rank_product(chosen_down, attention_output), SCALE * rank_product(chosen_up, grad_out)], 0
     )
-    for where in (SWAP_CORE, SWAP_LOW, *SWAP_Z):
+    for where in (SWAP_CORE, SWAP_LOW):
         sums = sums + permute(sums, where)
-    ranks = sums.astype(BF16)
+    far = permute(after(near, sums), SWAP_CORE)
+    gathered, sums = lax.optimization_barrier((gathered, sums))
+    rank_sums = jnp.sum(exchange(jnp.broadcast_to(sums[None], (RING,) + sums.shape), GROUPS_Z), 0)
+    partial_value = product(c.reshape(1), gathered.reshape(RING * half, 4 * width), near, far)
+    partial_value = after(partial_value, rank_sums)
+    spread = exchange(partial_value.reshape(RING, half, 4 * width), GROUPS_SCATTER)
+    total = jnp.sum(spread.astype(F32), 0).astype(BF16)
+
+    ranks = rank_sums.astype(BF16)
 
     def per_slot(value):
         spread_out = jnp.where(own_slot[:, None, :], value[None], jnp.zeros((), BF16))
@@ -208,15 +216,17 @@
     both = jnp.concatenate([terms, away], 1)
     owned = jnp.einsum("as,ksw->akw", hot, both, preferred_element_type=F32).astype(BF16)
     owned = owned.reshape(RING, own * 2 * RANK, width)
-    grads = jnp.sum(exchange(owned, GROUPS_Y).astype(F32), 0).reshape(own, 2, RANK, width)
 
     quarters = total.reshape(half, 2, 2, width)
     halves = total.reshape(half, 2, 2 * width)
-    out = []
+    sent = []
     for a in (0, 1):
         forward = jnp.where(flip, halves[:, 1 - a], halves[:, a])
         backward = quarters[:, :, a].reshape(half, 2 * width)
-        out.append(permute(jnp.where(first, forward, backward), FROM_BLOCKS[a]))
+        sent.append(jnp.where(first, forward, backward))
+    out = [permute(sent[a], FROM_BLOCKS[a]) for a in (0, 1)]
+    owned = after(owned, *sent)
+    grads = jnp.sum(exchange(owned, GROUPS_Y).astype(F32), 0).reshape(own, 2, RANK, width)
     back = jnp.where(first, z >> 2, xl)
     both_halves = jnp.concatenate(
         [jnp.where(back == 0, out[0], out[1]), jnp.where(back == 0, out[1], out[0])], 0

time: 179 us -> 156 us (0.87)
  the two profiles are of different devices: /device:TPU:57 before, /device:TPU:64 now
where the time goes in v2:
time: 156 us; the launch traced here: 155 us
  starting transfers between devices  88.9 us (57%)
  waiting for transfers between devices  43.8 us (28%)
  local copies, waits for them, and re-layouts  8.65 us (6%)
  other arithmetic  4.73 us (3%)
  Pallas kernels  4.54 us (3%)
  matrix products  2.84 us (2%)
    ppermute x14, starting transfers between devices, permute(): return lax.ppermute(value, AXES, where)  52.5 us
    all_to_all x5, starting transfers between devices, exchange(): lax.all_to_all(value, AXES, 0, 0, axis_index_groups=groups, tiled=True)  36.4 us
    all_to_all x5, waiting for transfers between devices, exchange(): lax.all_to_all(value, AXES, 0, 0, axis_index_groups=groups, tiled=True)  30.1 us
    ppermute x14, waiting for transfers between devices, permute(): return lax.ppermute(value, AXES, where)  13.7 us
    pallas_call x1, Pallas kernels, product(): pl.pallas_call(product_kernel, grid=(count // tile,), in_specs=[pl.BlockS...  4.54 us
  transfers between devices with their start and end apart: 19, of which 10 were waited for; matrix products, arithmetic and copies ran while one was open for 8% of the time, Pallas kernels for 3%

profile of v2, /device:TPU:64, one launch (start us, length us, event | category | flops | bytes accessed | tf_op | source)
XLA Modules:
  0.0 154.7 jit_solution(11559006157328792640)
XLA Ops:
  2.6 1.9 %collective-permute-start = (bf16[192,256]{1,0:T(8,128)(2,1)S(1)}, bf16[192,256]{1,0:T(8,128)(2,1)S(1)}, u32[]{:S(2)}, u32[]{:S(2)}) collective-permute-start(bf16[192,256]{1,0:T(8,128)(2,1)S(1)} %get-tuple-element.25), channel_id=1, source_target_pairs={{0,1},{1,0},{2,3},{3,2},{4,5},{5,4},{6,7},{7,6},{8,9},{9,8},{10,11... | collective-permute-start | bytes 294920 | tf_op jit(solution)/shard_map/ppermute | solution.py:79
  6.1 7.1 %all-to-all-start = ((bf16[8,128,256]{2,1,0:T(8,128)(2,1)}), bf16[8,128,256]{2,1,0:T(8,128)(2,1)S(1)}, u32[]{:S(2)}, u32[]{:S(2)}) async-start(bf16[8,128,256]{2,1,0:T(8,128)(2,1)} %broadcast_in_dim.112), calls=%async_computation | async-start | bytes 1048576 | tf_op jit(solution)/shard_map/all_to_all | solution.py:83
  14.2 4.9 %collective-permute-start.4 = (s32[1,6]{1,0:T(1,128)S(1)}, s32[1,6]{1,0:T(1,128)S(1)}, u32[]{:S(2)}, u32[]{:S(2)}) collective-permute-start(s32[1,6]{1,0:T(1,128)S(1)} %copy-done.4), channel_id=1, source_target_pairs={{0,256},{1,257},{2,258},{3,259},{4,260},{5,261},{6,262},{7,263},{8... | collective-permute-start | bytes 80 | tf_op jit(solution)/shard_map/ppermute | solution.py:79
  19.1 2.5 %collective-permute-start.2 = (bf16[96,512]{1,0:T(8,128)(2,1)S(1)}, bf16[96,512]{1,0:T(8,128)(2,1)S(1)}, u32[]{:S(2)}, u32[]{:S(2)}) collective-permute-start(bf16[96,512]{1,0:T(8,128)(2,1)S(1)} %get-tuple-element.33), channel_id=1, source_target_pairs={{0,2},{1,3},{2,0},{3,35},{4,6},{5,67},{6,4},{7,99},{8,10},{9,131},... | collective-permute-start | bytes 294920 | tf_op jit(solution)/shard_map/ppermute | solution.py:79
  21.6 3.3 %collective-permute-start.3 = (bf16[256,512]{1,0:T(8,128)(2,1)S(1)}, bf16[256,512]{1,0:T(8,128)(2,1)S(1)}, u32[]{:S(2)}, u32[]{:S(2)}) collective-permute-start(bf16[256,512]{1,0:T(8,128)(2,1)S(1)} %copy-done.1), channel_id=1, source_target_pairs={{0,2},{1,3},{2,0},{3,1},{4,6},{5,7},{6,4},{7,5},{8,10},{9,11},{10,... | collective-permute-start | bytes 786440 | tf_op jit(solution)/shard_map/ppermute | solution.py:79
  25.7 4.2 %collective-permute-done.3 = bf16[256,512]{1,0:T(8,128)(2,1)S(1)} collective-permute-done((bf16[256,512]{1,0:T(8,128)(2,1)S(1)}, bf16[256,512]{1,0:T(8,128)(2,1)S(1)}, u32[]{:S(2)}, u32[]{:S(2)}) %collective-permute-start.3) | collective-permute-done | bytes 262176 | tf_op jit(solution)/shard_map/ppermute | solution.py:79
  32.8 6.0 %all-to-all-start.1 = ((bf16[8,96,1024]{2,1,0:T(8,128)(2,1)}), bf16[8,96,1024]{2,1,0:T(8,128)(2,1)S(1)}, u32[]{:S(2)}, u32[]{:S(2)}) async-start(bf16[8,96,1024]{2,1,0:T(8,128)(2,1)} %broadcast_in_dim.113), calls=%async_computation.1 | async-start | bytes 3145728 | tf_op jit(solution)/shard_map/all_to_all | solution.py:83
  39.7 3.8 %collective-permute-start.5 = (bf16[192,256]{1,0:T(8,128)(2,1)S(1)}, bf16[192,256]{1,0:T(8,128)(2,1)S(1)}, u32[]{:S(2)}, u32[]{:S(2)}) collective-permute-start(bf16[192,256]{1,0:T(8,128)(2,1)S(1)} %bitcast_select_fusion.2), channel_id=1, source_target_pairs={{0,256},{1,257},{2,258},{3,259},{4,260},{5,261},{6,262},{7,263},{8... | collective-permute-start | bytes 294920 | tf_op jit(solution)/shard_map/ppermute | solution.py:79
  43.5 3.6 %collective-permute-start.8 = (bf16[512,512]{1,0:T(8,128)(2,1)S(1)}, bf16[512,512]{1,0:T(8,128)(2,1)}, u32[]{:S(2)}, u32[]{:S(2)}) collective-permute-start(bf16[512,512]{1,0:T(8,128)(2,1)S(1)} %constant_dynamic-update-slice_fusion), channel_id=1, source_target_pairs={{0,256},{1,257},{2,258},{3,259},{4,260},{5,261},{6,262},{7,263},{8... | collective-permute-start | bytes 1572872 | tf_op jit(solution)/shard_map/ppermute | solution.py:79
  48.3 11.2 %collective-permute-start.6 = (f32[32,192]{1,0:T(8,128)S(1)}, f32[32,192]{1,0:T(8,128)S(1)}, u32[]{:S(2)}, u32[]{:S(2)}) collective-permute-start(f32[32,192]{1,0:T(8,128)S(1)} %pad_maximum_fusion.4), channel_id=1, source_target_pairs={{0,1},{1,0},{2,3},{3,2},{4,5},{5,4},{6,7},{7,6},{8,9},{9,8},{10,11... | collective-permute-start | bytes 73736 | tf_op jit(solution)/shard_map/ppermute | solution.py:79
  60.3 2.6 %collective-permute-start.7 = (f32[32,192]{1,0:T(8,128)S(1)}, f32[32,192]{1,0:T(8,128)S(1)}, u32[]{:S(2)}, u32[]{:S(2)}) collective-permute-start(f32[32,192]{1,0:T(8,128)S(1)} %fusion.38), channel_id=1, source_target_pairs={{0,2},{1,3},{2,0},{3,1},{4,6},{5,7},{6,4},{7,5},{8,10},{9,11},{10,... | collective-permute-start | bytes 73736 | tf_op jit(solution)/shard_map/ppermute | solution.py:79
  64.0 2.0 %collective-permute-done.7 = f32[32,192]{1,0:T(8,128)S(1)} collective-permute-done((f32[32,192]{1,0:T(8,128)S(1)}, f32[32,192]{1,0:T(8,128)S(1)}, u32[]{:S(2)}, u32[]{:S(2)}) %collective-permute-start.7) | collective-permute-done | bytes 24608 | tf_op jit(solution)/shard_map/ppermute | solution.py:79
  66.1 2.1 %collective-permute-start.9 = (bf16[512,1024]{1,0:T(8,128)(2,1)S(1)}, bf16[512,1024]{1,0:T(8,128)(2,1)}, u32[]{:S(2)}, u32[]{:S(2)}) collective-permute-start(bf16[512,1024]{1,0:T(8,128)(2,1)S(1)} %pad_maximum_fusion.near_ref), channel_id=1, source_target_pairs={{0,1},{1,0},{2,3},{3,2},{4,5},{5,4},{6,7},{7,6},{8,9},{9,8},{10,11... | collective-permute-start | bytes 3145736 | tf_op jit(solution)/shard_map/ppermute | solution.py:79
  68.9 11.1 %all-to-all-start.2 = ((f32[8,32,192]{2,1,0:T(8,128)}), f32[8,32,192]{2,1,0:T(8,128)S(1)}, u32[]{:S(2)}, u32[]{:S(2)}) async-start(f32[8,32,192]{2,1,0:T(8,128)} %broadcast_in_dim.121), calls=%async_computation.2 | async-start | bytes 524288 | tf_op jit(solution)/shard_map/all_to_all | solution.py:83
  80.0 4.5 %shard_map.102 = bf16[768,1024]{1,0:T(8,128)(2,1)} custom-call(s32[1]{0:T(128)} %bitcast.core_ref, bf16[768,1024]{1,0:T(8,128)(2,1)S(1)} %bitcast.69, bf16[512,1024]{1,0:T(8,128)(2,1)S(1)} %pad_maximum_fusion.near_ref, bf16[512,1024]{1,0:T(8,128)(2,1)} %collective-permute-done.9.far_ref), custom_call_target="tpu_custom_call" | custom-call | flops 1610612736 | bytes 5242880 | tf_op jit(solution)/shard_map/pallas_call | solution.py:113
  84.5 6.1 %all-to-all-done.2 = f32[8,32,192]{2,1,0:T(8,128)S(1)} async-done(((f32[8,32,192]{2,1,0:T(8,128)}), f32[8,32,192]{2,1,0:T(8,128)S(1)}, u32[]{:S(2)}, u32[]{:S(2)}) %all-to-all-start.2) | async-done | bytes 196640 | tf_op jit(solution)/shard_map/all_to_all | solution.py:83
  90.6 5.1 %all-to-all-start.3 = ((bf16[8,96,1024]{2,1,0:T(8,128)(2,1)}), bf16[8,96,1024]{2,1,0:T(8,128)(2,1)S(1)}, u32[]{:S(2)}, u32[]{:S(2)}) async-start(bf16[8,96,1024]{2,1,0:T(8,128)(2,1)} %bitcast.19), calls=%async_computation.3 | async-start | bytes 3145728 | tf_op jit(solution)/shard_map/all_to_all | solution.py:83
  96.1 3.2 %collective-permute-start.13 = (bf16[192,256]{1,0:T(8,128)(2,1)S(1)}, bf16[192,256]{1,0:T(8,128)(2,1)S(1)}, u32[]{:S(2)}, u32[]{:S(2)}) collective-permute-start(bf16[192,256]{1,0:T(8,128)(2,1)S(1)} %bitcast.82), channel_id=1, source_target_pairs={{0,256},{1,257},{2,258},{3,259},{4,260},{5,261},{6,262},{7,263},{8... | collective-permute-start | bytes 294920 | tf_op jit(solution)/shard_map/ppermute | solution.py:79
  99.6 4.7 %collective-permute-done.13 = bf16[192,256]{1,0:T(8,128)(2,1)S(1)} collective-permute-done((bf16[192,256]{1,0:T(8,128)(2,1)S(1)}, bf16[192,256]{1,0:T(8,128)(2,1)S(1)}, u32[]{:S(2)}, u32[]{:S(2)}) %collective-permute-start.13) | collective-permute-done | bytes 98336 | tf_op jit(solution)/shard_map/ppermute | solution.py:79
  104.5 14.2 %all-to-all-done.3 = bf16[8,96,1024]{2,1,0:T(8,128)(2,1)S(1)} async-done(((bf16[8,96,1024]{2,1,0:T(8,128)(2,1)}), bf16[8,96,1024]{2,1,0:T(8,128)(2,1)S(1)}, u32[]{:S(2)}, u32[]{:S(2)}) %all-to-all-start.3) | async-done | bytes 1572896 | tf_op jit(solution)/shard_map/all_to_all | solution.py:83
  120.6 4.1 %collective-permute-start.10 = (bf16[96,512]{1,0:T(8,128)(2,1)S(1)}, bf16[96,512]{1,0:T(8,128)(2,1)S(1)}, u32[]{:S(2)}, u32[]{:S(2)}) collective-permute-start(bf16[96,512]{1,0:T(8,128)(2,1)S(1)} %get-tuple-element.22), channel_id=1, source_target_pairs={{0,0},{1,1},{2,16},{3,3},{4,32},{5,5},{6,48},{7,7},{8,64},{9,9},{1... | collective-permute-start | bytes 294920 | tf_op jit(solution)/shard_map/ppermute | solution.py:79
  124.8 6.8 %collective-permute-start.11 = (bf16[96,512]{1,0:T(8,128)(2,1)S(1)}, bf16[96,512]{1,0:T(8,128)(2,1)S(1)}, u32[]{:S(2)}, u32[]{:S(2)}) collective-permute-start(bf16[96,512]{1,0:T(8,128)(2,1)S(1)} %get-tuple-element.23), channel_id=1, source_target_pairs={{0,16},{1,3},{2,0},{3,1},{4,48},{5,7},{6,32},{7,5},{8,80},{9,11},{... | collective-permute-start | bytes 294920 | tf_op jit(solution)/shard_map/ppermute | solution.py:79
  133.6 7.1 %all-to-all-start.4 = ((bf16[8,128,256]{2,1,0:T(8,128)(2,1)}), bf16[8,128,256]{2,1,0:T(8,128)(2,1)S(1)}, u32[]{:S(2)}, u32[]{:S(2)}) async-start(bf16[8,128,256]{2,1,0:T(8,128)(2,1)} %reshape.533), calls=%async_computation.4 | async-start | bytes 1048576 | tf_op jit(solution)/shard_map/all_to_all | solution.py:83
  145.7 8.3 %all-to-all-done.4 = bf16[8,128,256]{2,1,0:T(8,128)(2,1)S(1)} async-done(((bf16[8,128,256]{2,1,0:T(8,128)(2,1)}), bf16[8,128,256]{2,1,0:T(8,128)(2,1)S(1)}, u32[]{:S(2)}, u32[]{:S(2)}) %all-to-all-start.4) | async-done | bytes 524320 | tf_op jit(solution)/shard_map/all_to_all | solution.py:83
  (88 shorter events, 23.1 us)
Async XLA Ops:
  0.6 12.6 %copy-start.4 = (s32[1,6]{1,0:T(1,128)S(1)}, s32[1,6]{1,0:T(1,128)}, u32[]{:S(2)}) copy-start(s32[1,6]{1,0:T(1,128)} %param.11) | copy-start | bytes 76
  0.6 13.5 %copy-start.1 = (bf16[256,512]{1,0:T(8,128)(2,1)S(1)}, bf16[256,512]{1,0:T(8,128)(2,1)}, u32[]{:S(2)}) copy-start(bf16[256,512]{1,0:T(8,128)(2,1)} %param.8) | copy-start | bytes 786436
  2.6 10.8 %collective-permute-start = (bf16[192,256]{1,0:T(8,128)(2,1)S(1)}, bf16[192,256]{1,0:T(8,128)(2,1)S(1)}, u32[]{:S(2)}, u32[]{:S(2)}) collective-permute-start(bf16[192,256]{1,0:T(8,128)(2,1)S(1)} %get-tuple-element.25), channel_id=1, source_target_pairs={{0,1},{1,0},{2,3},{3,2},{4,5},{5,4},{6,7},{7,6},{8,9},{9,8},{10,11... | collective-permute-start | bytes 294920 | tf_op jit(solution)/shard_map/ppermute | solution.py:79
  6.1 25.3 %all-to-all-start = ((bf16[8,128,256]{2,1,0:T(8,128)(2,1)}), bf16[8,128,256]{2,1,0:T(8,128)(2,1)S(1)}, u32[]{:S(2)}, u32[]{:S(2)}) async-start(bf16[8,128,256]{2,1,0:T(8,128)(2,1)} %broadcast_in_dim.112), calls=%async_computation | async-start | bytes 1048576 | tf_op jit(solution)/shard_map/all_to_all | solution.py:83
  13.5 11.5 %collective-permute-start.1 = (bf16[96,512]{1,0:T(8,128)(2,1)S(1)}, bf16[96,512]{1,0:T(8,128)(2,1)S(1)}, u32[]{:S(2)}, u32[]{:S(2)}) collective-permute-start(bf16[96,512]{1,0:T(8,128)(2,1)S(1)} %get-tuple-element.32), channel_id=1, source_target_pairs={{0,0},{1,1},{2,2},{3,33},{4,4},{5,65},{6,6},{7,97},{8,8},{9,129},{... | collective-permute-start | bytes 294920 | tf_op jit(solution)/shard_map/ppermute | solution.py:79
  14.2 24.6 %collective-permute-start.4 = (s32[1,6]{1,0:T(1,128)S(1)}, s32[1,6]{1,0:T(1,128)S(1)}, u32[]{:S(2)}, u32[]{:S(2)}) collective-permute-start(s32[1,6]{1,0:T(1,128)S(1)} %copy-done.4), channel_id=1, source_target_pairs={{0,256},{1,257},{2,258},{3,259},{4,260},{5,261},{6,262},{7,263},{8... | collective-permute-start | bytes 80 | tf_op jit(solution)/shard_map/ppermute | solution.py:79
  19.1 6.5 %collective-permute-start.2 = (bf16[96,512]{1,0:T(8,128)(2,1)S(1)}, bf16[96,512]{1,0:T(8,128)(2,1)S(1)}, u32[]{:S(2)}, u32[]{:S(2)}) collective-permute-start(bf16[96,512]{1,0:T(8,128)(2,1)S(1)} %get-tuple-element.33), channel_id=1, source_target_pairs={{0,2},{1,3},{2,0},{3,35},{4,6},{5,67},{6,4},{7,99},{8,10},{9,131},... | collective-permute-start | bytes 294920 | tf_op jit(solution)/shard_map/ppermute | solution.py:79
  21.6 8.3 %collective-permute-start.3 = (bf16[256,512]{1,0:T(8,128)(2,1)S(1)}, bf16[256,512]{1,0:T(8,128)(2,1)S(1)}, u32[]{:S(2)}, u32[]{:S(2)}) collective-permute-start(bf16[256,512]{1,0:T(8,128)(2,1)S(1)} %copy-done.1), channel_id=1, source_target_pairs={{0,2},{1,3},{2,0},{3,1},{4,6},{5,7},{6,4},{7,5},{8,10},{9,11},{10,... | collective-permute-start | bytes 786440 | tf_op jit(solution)/shard_map/ppermute | solution.py:79
  32.8 15.0 %copy-start.2 = (bf16[192,256]{1,0:T(8,128)(2,1)S(1)}, bf16[192,256]{1,0:T(8,128)(2,1)}, u32[]{:S(2)}) copy-start(bf16[192,256]{1,0:T(8,128)(2,1)} %param.13) | copy-start | bytes 294916
  32.8 35.4 %all-to-all-start.1 = ((bf16[8,96,1024]{2,1,0:T(8,128)(2,1)}), bf16[8,96,1024]{2,1,0:T(8,128)(2,1)S(1)}, u32[]{:S(2)}, u32[]{:S(2)}) async-start(bf16[8,96,1024]{2,1,0:T(8,128)(2,1)} %broadcast_in_dim.113), calls=%async_computation.1 | async-start | bytes 3145728 | tf_op jit(solution)/shard_map/all_to_all | solution.py:83
  38.8 9.3 %copy-start = (bf16[192,256]{1,0:T(8,128)(2,1)S(1)}, bf16[192,256]{1,0:T(8,128)(2,1)}, u32[]{:S(2)}) copy-start(bf16[192,256]{1,0:T(8,128)(2,1)} %param.7) | copy-start | bytes 294916
  39.7 8.0 %collective-permute-start.5 = (bf16[192,256]{1,0:T(8,128)(2,1)S(1)}, bf16[192,256]{1,0:T(8,128)(2,1)S(1)}, u32[]{:S(2)}, u32[]{:S(2)}) collective-permute-start(bf16[192,256]{1,0:T(8,128)(2,1)S(1)} %bitcast_select_fusion.2), channel_id=1, source_target_pairs={{0,256},{1,257},{2,258},{3,259},{4,260},{5,261},{6,262},{7,263},{8... | collective-permute-start | bytes 294920 | tf_op jit(solution)/shard_map/ppermute | solution.py:79
  43.5 19.4 %collective-permute-start.8 = (bf16[512,512]{1,0:T(8,128)(2,1)S(1)}, bf16[512,512]{1,0:T(8,128)(2,1)}, u32[]{:S(2)}, u32[]{:S(2)}) collective-permute-start(bf16[512,512]{1,0:T(8,128)(2,1)S(1)} %constant_dynamic-update-slice_fusion), channel_id=1, source_target_pairs={{0,256},{1,257},{2,258},{3,259},{4,260},{5,261},{6,262},{7,263},{8... | collective-permute-start | bytes 1572872 | tf_op jit(solution)/shard_map/ppermute | solution.py:79
  48.3 12.0 %collective-permute-start.6 = (f32[32,192]{1,0:T(8,128)S(1)}, f32[32,192]{1,0:T(8,128)S(1)}, u32[]{:S(2)}, u32[]{:S(2)}) collective-permute-start(f32[32,192]{1,0:T(8,128)S(1)} %pad_maximum_fusion.4), channel_id=1, source_target_pairs={{0,1},{1,0},{2,3},{3,2},{4,5},{5,4},{6,7},{7,6},{8,9},{9,8},{10,11... | collective-permute-start | bytes 73736 | tf_op jit(solution)/shard_map/ppermute | solution.py:79
  60.3 5.8 %collective-permute-start.7 = (f32[32,192]{1,0:T(8,128)S(1)}, f32[32,192]{1,0:T(8,128)S(1)}, u32[]{:S(2)}, u32[]{:S(2)}) collective-permute-start(f32[32,192]{1,0:T(8,128)S(1)} %fusion.38), channel_id=1, source_target_pairs={{0,2},{1,3},{2,0},{3,1},{4,6},{5,7},{6,4},{7,5},{8,10},{9,11},{10,... | collective-permute-start | bytes 73736 | tf_op jit(solution)/shard_map/ppermute | solution.py:79
  66.1 13.9 %collective-permute-start.9 = (bf16[512,1024]{1,0:T(8,128)(2,1)S(1)}, bf16[512,1024]{1,0:T(8,128)(2,1)}, u32[]{:S(2)}, u32[]{:S(2)}) collective-permute-start(bf16[512,1024]{1,0:T(8,128)(2,1)S(1)} %pad_maximum_fusion.near_ref), channel_id=1, source_target_pairs={{0,1},{1,0},{2,3},{3,2},{4,5},{5,4},{6,7},{7,6},{8,9},{9,8},{10,11... | collective-permute-start | bytes 3145736 | tf_op jit(solution)/shard_map/ppermute | solution.py:79
  68.9 21.7 %all-to-all-start.2 = ((f32[8,32,192]{2,1,0:T(8,128)}), f32[8,32,192]{2,1,0:T(8,128)S(1)}, u32[]{:S(2)}, u32[]{:S(2)}) async-start(f32[8,32,192]{2,1,0:T(8,128)} %broadcast_in_dim.121), calls=%async_computation.2 | async-start | bytes 524288 | tf_op jit(solution)/shard_map/all_to_all | solution.py:83
  90.6 5.3 %copy-start.3 = (bf16[192,256]{1,0:T(8,128)(2,1)S(1)}, bf16[192,256]{1,0:T(8,128)(2,1)}, u32[]{:S(2)}) copy-start(bf16[192,256]{1,0:T(8,128)(2,1)} %param.13) | copy-start | bytes 294916
  90.6 28.1 %all-to-all-start.3 = ((bf16[8,96,1024]{2,1,0:T(8,128)(2,1)}), bf16[8,96,1024]{2,1,0:T(8,128)(2,1)S(1)}, u32[]{:S(2)}, u32[]{:S(2)}) async-start(bf16[8,96,1024]{2,1,0:T(8,128)(2,1)} %bitcast.19), calls=%async_computation.3 | async-start | bytes 3145728 | tf_op jit(solution)/shard_map/all_to_all | solution.py:83
  96.1 8.2 %collective-permute-start.13 = (bf16[192,256]{1,0:T(8,128)(2,1)S(1)}, bf16[192,256]{1,0:T(8,128)(2,1)S(1)}, u32[]{:S(2)}, u32[]{:S(2)}) collective-permute-start(bf16[192,256]{1,0:T(8,128)(2,1)S(1)} %bitcast.82), channel_id=1, source_target_pairs={{0,256},{1,257},{2,258},{3,259},{4,260},{5,261},{6,262},{7,263},{8... | collective-permute-start | bytes 294920 | tf_op jit(solution)/shard_map/ppermute | solution.py:79
  120.6 20.1 %collective-permute-start.10 = (bf16[96,512]{1,0:T(8,128)(2,1)S(1)}, bf16[96,512]{1,0:T(8,128)(2,1)S(1)}, u32[]{:S(2)}, u32[]{:S(2)}) collective-permute-start(bf16[96,512]{1,0:T(8,128)(2,1)S(1)} %get-tuple-element.22), channel_id=1, source_target_pairs={{0,0},{1,1},{2,16},{3,3},{4,32},{5,5},{6,48},{7,7},{8,64},{9,9},{1... | collective-permute-start | bytes 294920 | tf_op jit(solution)/shard_map/ppermute | solution.py:79
  124.8 16.0 %collective-permute-start.11 = (bf16[96,512]{1,0:T(8,128)(2,1)S(1)}, bf16[96,512]{1,0:T(8,128)(2,1)S(1)}, u32[]{:S(2)}, u32[]{:S(2)}) collective-permute-start(bf16[96,512]{1,0:T(8,128)(2,1)S(1)} %get-tuple-element.23), channel_id=1, source_target_pairs={{0,16},{1,3},{2,0},{3,1},{4,48},{5,7},{6,32},{7,5},{8,80},{9,11},{... | collective-permute-start | bytes 294920 | tf_op jit(solution)/shard_map/ppermute | solution.py:79
  133.6 20.4 %all-to-all-start.4 = ((bf16[8,128,256]{2,1,0:T(8,128)(2,1)}), bf16[8,128,256]{2,1,0:T(8,128)(2,1)S(1)}, u32[]{:S(2)}, u32[]{:S(2)}) async-start(bf16[8,128,256]{2,1,0:T(8,128)(2,1)} %reshape.533), calls=%async_computation.4 | async-start | bytes 1048576 | tf_op jit(solution)/shard_map/all_to_all | solution.py:83
  140.8 3.2 %collective-permute-start.12 = (bf16[192,256]{1,0:T(8,128)(2,1)S(1)}, bf16[192,256]{1,0:T(8,128)(2,1)S(1)}, u32[]{:S(2)}, u32[]{:S(2)}) collective-permute-start(bf16[192,256]{1,0:T(8,128)(2,1)S(1)} %pad_maximum_fusion.1), channel_id=1, source_target_pairs={{0,1},{1,0},{2,3},{3,2},{4,5},{5,4},{6,7},{7,6},{8,9},{9,8},{10,11... | collective-permute-start | bytes 294920 | tf_op jit(solution)/shard_map/ppermute | solution.py:79

commit v3 on v2

--- a/solution.py
+++ b/solution.py
@@ -83,8 +83,7 @@
     return lax.all_to_all(value, AXES, 0, 0, axis_index_groups=groups, tiled=True)
 
 
-def after(value, *others):
-    return lax.optimization_barrier((value, *others))[0]
+together = lax.optimization_barrier
 
 
 def product_kernel(core_ref, rows_ref, near_ref, far_ref, out_ref):
@@ -137,18 +136,20 @@
     own = down_maps.shape[0]
 
     slots = adapter_index[0]
-    table = jnp.stack([down_maps, up_maps])
-    tables = exchange(jnp.broadcast_to(table[None], (RING,) + table.shape).reshape(RING, -1, width), GROUPS_Y)
-    tables = tables.reshape(RING, 2, own, RANK, width)
 
     positions = lax.iota(jnp.int32, SLOT_LEN)
     live = (positions[None, :] < lengths[0][:, None]).astype(BF16)
-    grad_out = (cotangent.reshape(SLOTS, SLOT_LEN, width) * live[:, :, None]).reshape(tokens, width)
-    mine = jnp.where(first, attention_output, grad_out)
-    theirs = permute(jnp.where(first, grad_out, attention_output), SWAP_CORE)
+    live = live.reshape(tokens, 1)
+    grad_out = cotangent * live
+    forward = jnp.concatenate([attention_output, down_maps.reshape(-1, width)], 0)
+    backward = jnp.concatenate([cotangent, up_maps.reshape(-1, width)], 0)
+    mine = jnp.where(first, forward, backward)
+    theirs = permute(jnp.where(first, backward, forward), SWAP_CORE)
     pair = jnp.where(first, jnp.concatenate([mine, theirs], 1), jnp.concatenate([theirs, mine], 1))
-    other_slots = permute(after(adapter_index, pair), SWAP_HIGH)[0]
-    near_rows = permute(after(output_weight, pair), SWAP_LOW)
+    pair, table = pair[:tokens] * jnp.where(first, jnp.ones((), BF16), live), pair[tokens:]
+
+    tables = exchange(jnp.broadcast_to(table[None], (RING,) + table.shape), GROUPS_Y)
+    tables = tables.reshape(RING, own, RANK, 2 * width)
     side = jnp.where(first, xl, z >> 2)
     top, bottom = pair[:half], pair[half:]
     got = [
@@ -159,51 +160,54 @@
     rows_x = jnp.concatenate([got[0][:, :width], got[1][:, :width], got[0][:, width:], got[1][:, width:]], 1)
     rows_g = jnp.concatenate([jnp.where(flip, got[1], got[0]), jnp.where(flip, got[0], got[1])], 1)
     rows = jnp.where(first, rows_x, rows_g)
-    rows = after(rows, near_rows, tables, other_slots)
+    block = jnp.concatenate([output_weight, permute(output_weight, SWAP_LOW)], 0)
+    numbers = jnp.pad(slots.astype(BF16), (0, 8 - SLOTS))
+    numbers = jnp.broadcast_to(numbers[:, None], (8, block.shape[1]))
+    came = permute(jnp.concatenate([block, numbers], 0), SWAP_HIGH)
+    near = jnp.concatenate([block, came[:-8]], 1)
+    other_slots = came[-8:, 0][:SLOTS].astype(jnp.int32)
+    rows, near, tables, other_slots = together((rows, near, tables, other_slots))
     gathered = exchange(jnp.broadcast_to(rows[None], (RING,) + rows.shape), GROUPS_GATHER)
 
-    block = jnp.concatenate([output_weight, near_rows], 0)
-    near = jnp.concatenate([block, permute(block, SWAP_HIGH)], 1)
     def pick(which):
         local = which % (RING * own)
-        return tables[local // own, :, local % own]
+        return tables[local // own, local % own]
 
     high = slots // (RING * own)
     other_high = other_slots // (RING * own)
-    give = jnp.where((other_high == xh)[:, None, None, None], pick(other_slots), 0)
-    take = permute(give.reshape(-1, width), SWAP_HIGH).reshape(SLOTS, 2, RANK, width)
-    chosen = jnp.where((high == xh)[:, None, None, None], pick(slots), take)
-    chosen_down = chosen[:, 0].reshape(SLOTS * RANK, width)
-    chosen_up = chosen[:, 1].reshape(SLOTS * RANK, width)
+    give = jnp.where((other_high == xh)[:, None, None], pick(other_slots), 0)
+    take = permute(give.reshape(-1, 2 * width), SWAP_HIGH).reshape(give.shape)
+    chosen = jnp.where((high == xh)[:, None, None], pick(slots), take).reshape(SLOTS * RANK, 2 * width)
 
     own_slot = (lax.iota(jnp.int32, tokens)[None, :] // SLOT_LEN) == lax.iota(jnp.int32, SLOTS)[:, None]
     contract = (((1,), (1,)), ((), ()))
 
-    def rank_product(maps, values):
-        every = lax.dot_general(maps, values, contract, preferred_element_type=F32)
-        every = every.reshape(SLOTS, RANK, tokens)
-        return jnp.sum(jnp.where(own_slot[:, None, :], every, 0.0), 0)
-
-    sums = jnp.concatenate(
-        [rank_product(chosen_down, attention_output), SCALE * rank_product(chosen_up, grad_out)], 0
-    )
-    for where in (SWAP_CORE, SWAP_LOW):
-        sums = sums + permute(sums, where)
-    far = permute(after(near, sums), SWAP_CORE)
-    gathered, sums = lax.optimization_barrier((gathered, sums))
+    every = lax.dot_general(chosen, pair, contract, preferred_element_type=F32)
+    sums = jnp.sum(jnp.where(own_slot[:, None, :], every.reshape(SLOTS, RANK, tokens), 0.0), 0)
+    sums = sums + permute(sums, SWAP_LOW)
+    near, sums = together((near, sums))
+    far = permute(near, SWAP_CORE)
+    gathered, sums = together((gathered, sums))
     rank_sums = jnp.sum(exchange(jnp.broadcast_to(sums[None], (RING,) + sums.shape), GROUPS_Z), 0)
     partial_value = product(c.reshape(1), gathered.reshape(RING * half, 4 * width), near, far)
-    partial_value = after(partial_value, rank_sums)
+    partial_value, rank_sums = together((partial_value, rank_sums))
     spread = exchange(partial_value.reshape(RING, half, 4 * width), GROUPS_SCATTER)
     total = jnp.sum(spread.astype(F32), 0).astype(BF16)
 
-    ranks = rank_sums.astype(BF16)
+    ranks = jnp.where(first, rank_sums, SCALE * rank_sums).astype(BF16)
+
+    own_columns = jnp.where(first, chosen[:, :width], chosen[:, width:])
+    their_columns = jnp.where(first, chosen[:, width:], chosen[:, :width])
+    came = permute(jnp.concatenate([jnp.pad(ranks, ((0, 0), (0, width - tokens))), their_columns], 0), SWAP_CORE)
+    other_ranks, other_columns = came[:RANK, :tokens], came[RANK:]
+    chosen_down, chosen_up = jnp.where(first, own_columns, other_columns), jnp.where(first, other_columns, own_columns)
 
     def per_slot(value):
         spread_out = jnp.where(own_slot[:, None, :], value[None], jnp.zeros((), BF16))
         return spread_out.reshape(SLOTS * RANK, tokens)
 
-    middle, grad_middle = per_slot(ranks[:RANK]), per_slot(ranks[RANK:])
+    middle = per_slot(jnp.where(first, ranks, other_ranks))
+    grad_middle = per_slot(jnp.where(first, other_ranks, ranks))
 
     up_terms = (SCALE * jnp.dot(middle, grad_out, preferred_element_type=F32)).astype(BF16)
     down_terms = jnp.dot(grad_middle, attention_output, preferred_element_type=F32).astype(BF16)
@@ -224,8 +228,8 @@
         forward = jnp.where(flip, halves[:, 1 - a], halves[:, a])
         backward = quarters[:, :, a].reshape(half, 2 * width)
         sent.append(jnp.where(first, forward, backward))
+    owned, *sent = together((owned, *sent))
     out = [permute(sent[a], FROM_BLOCKS[a]) for a in (0, 1)]
-    owned = after(owned, *sent)
     grads = jnp.sum(exchange(owned, GROUPS_Y).astype(F32), 0).reshape(own, 2, RANK, width)
     back = jnp.where(first, z >> 2, xl)
     both_halves = jnp.concatenate(

time: 156 us -> 149 us (0.955)
  the two profiles are of different devices: /device:TPU:64 before, /device:TPU:6 now
where the time goes in v3:
time: 149 us; the launch traced here: 148 us
  starting transfers between devices  80 us (54%)
  waiting for transfers between devices  44.9 us (30%)
  local copies, waits for them, and re-layouts  8.72 us (6%)
  other arithmetic  5.53 us (4%)
  Pallas kernels  4.55 us (3%)
  matrix products  2.61 us (2%)
    all_to_all x5, starting transfers between devices, exchange(): lax.all_to_all(value, AXES, 0, 0, axis_index_groups=groups, tiled=True)  40.6 us
    ppermute x13, starting transfers between devices, permute(): return lax.ppermute(value, AXES, where)  39.4 us
    ppermute x13, waiting for transfers between devices, permute(): return lax.ppermute(value, AXES, where)  23.1 us
    all_to_all x5, waiting for transfers between devices, exchange(): lax.all_to_all(value, AXES, 0, 0, axis_index_groups=groups, tiled=True)  21.9 us
    pallas_call x1, Pallas kernels, product(): pl.pallas_call(product_kernel, grid=(count // tile,), in_specs=[pl.BlockS...  4.55 us
  transfers between devices with their start and end apart: 18, of which 12 were waited for; matrix products, arithmetic and copies ran while one was open for 8% of the time, Pallas kernels for 3%

profile of v3, /device:TPU:6, one launch (start us, length us, event | category | flops | bytes accessed | tf_op | source)
XLA Modules:
  0.0 147.6 jit_solution(12517925794081208824)
XLA Ops:
  1.7 1.9 %collective-permute-start = (bf16[256,256]{1,0:T(8,128)(2,1)S(1)}, bf16[256,256]{1,0:T(8,128)(2,1)S(1)}, u32[]{:S(2)}, u32[]{:S(2)}) collective-permute-start(bf16[256,256]{1,0:T(8,128)(2,1)S(1)} %get-tuple-element.35), channel_id=1, source_target_pairs={{0,1},{1,0},{2,3},{3,2},{4,5},{5,4},{6,7},{7,6},{8,9},{9,8},{10,11... | collective-permute-start | bytes 393224 | tf_op jit(solution)/shard_map/ppermute | solution.py:79
  3.6 2.7 %collective-permute-start.3 = (bf16[256,512]{1,0:T(8,128)(2,1)}, bf16[256,512]{1,0:T(8,128)(2,1)S(1)}, u32[]{:S(2)}, u32[]{:S(2)}) collective-permute-start(bf16[256,512]{1,0:T(8,128)(2,1)} %param.8), channel_id=1, source_target_pairs={{0,2},{1,3},{2,0},{3,1},{4,6},{5,7},{6,4},{7,5},{8,10},{9,11},{10,... | collective-permute-start | bytes 786440 | tf_op jit(solution)/shard_map/ppermute | solution.py:79
  8.1 3.1 %collective-permute-start.2 = (bf16[96,512]{1,0:T(8,128)(2,1)S(1)}, bf16[96,512]{1,0:T(8,128)(2,1)S(1)}, u32[]{:S(2)}, u32[]{:S(2)}) collective-permute-start(bf16[96,512]{1,0:T(8,128)(2,1)S(1)} %get-tuple-element.43), channel_id=1, source_target_pairs={{0,2},{1,3},{2,0},{3,35},{4,6},{5,67},{6,4},{7,99},{8,10},{9,131},... | collective-permute-start | bytes 294920 | tf_op jit(solution)/shard_map/ppermute | solution.py:79
  12.8 7.1 %all-to-all-start = ((bf16[8,64,512]{2,1,0:T(8,128)(2,1)}), bf16[8,64,512]{2,1,0:T(8,128)(2,1)S(1)}, u32[]{:S(2)}, u32[]{:S(2)}) async-start(bf16[8,64,512]{2,1,0:T(8,128)(2,1)} %broadcast_in_dim.122), calls=%async_computation | async-start | bytes 1048576 | tf_op jit(solution)/shard_map/all_to_all | solution.py:83
  20.2 4.1 %collective-permute-start.4 = (bf16[520,512]{1,0:T(8,128)(2,1)S(1)}, bf16[520,512]{1,0:T(8,128)(2,1)S(1)}, u32[]{:S(2)}, u32[]{:S(2)}) collective-permute-start(bf16[520,512]{1,0:T(8,128)(2,1)S(1)} %maximum_maximum_fusion), channel_id=1, source_target_pairs={{0,256},{1,257},{2,258},{3,259},{4,260},{5,261},{6,262},{7,263},{8... | collective-permute-start | bytes 1597448 | tf_op jit(solution)/shard_map/ppermute | solution.py:79
  24.3 8.5 %collective-permute-done.4 = bf16[520,512]{1,0:T(8,128)(2,1)S(1)} collective-permute-done((bf16[520,512]{1,0:T(8,128)(2,1)S(1)}, bf16[520,512]{1,0:T(8,128)(2,1)S(1)}, u32[]{:S(2)}, u32[]{:S(2)}) %collective-permute-start.4) | collective-permute-done | bytes 532512 | tf_op jit(solution)/shard_map/ppermute | solution.py:79
  34.9 7.8 %all-to-all-start.1 = ((bf16[8,96,1024]{2,1,0:T(8,128)(2,1)}), bf16[8,96,1024]{2,1,0:T(8,128)(2,1)S(1)}, u32[]{:S(2)}, u32[]{:S(2)}) async-start(bf16[8,96,1024]{2,1,0:T(8,128)(2,1)} %broadcast_in_dim.124), calls=%async_computation.1 | async-start | bytes 3145728 | tf_op jit(solution)/shard_map/all_to_all | solution.py:83
  43.6 2.8 %collective-permute-start.5 = (bf16[96,512]{1,0:T(8,128)(2,1)S(1)}, bf16[96,512]{1,0:T(8,128)(2,1)}, u32[]{:S(2)}, u32[]{:S(2)}) collective-permute-start(bf16[96,512]{1,0:T(8,128)(2,1)S(1)} %bitcast_select_fusion.2), channel_id=1, source_target_pairs={{0,256},{1,257},{2,258},{3,259},{4,260},{5,261},{6,262},{7,263},{8... | collective-permute-start | bytes 294920 | tf_op jit(solution)/shard_map/ppermute | solution.py:79
  47.9 3.9 %collective-permute-done.5 = bf16[96,512]{1,0:T(8,128)(2,1)} collective-permute-done((bf16[96,512]{1,0:T(8,128)(2,1)S(1)}, bf16[96,512]{1,0:T(8,128)(2,1)}, u32[]{:S(2)}, u32[]{:S(2)}) %collective-permute-start.5) | collective-permute-done | bytes 98336 | tf_op jit(solution)/shard_map/ppermute | solution.py:79
  52.9 6.9 %collective-permute-start.6 = (f32[16,192]{1,0:T(8,128)S(1)}, f32[16,192]{1,0:T(8,128)S(1)}, u32[]{:S(2)}, u32[]{:S(2)}) collective-permute-start(f32[16,192]{1,0:T(8,128)S(1)} %fusion.1), channel_id=1, source_target_pairs={{0,2},{1,3},{2,0},{3,1},{4,6},{5,7},{6,4},{7,5},{8,10},{9,11},{10,... | collective-permute-start | bytes 36872 | tf_op jit(solution)/shard_map/ppermute | solution.py:79
  61.6 4.8 %collective-permute-start.7 = (bf16[512,1024]{1,0:T(8,128)(2,1)S(1)}, bf16[512,1024]{1,0:T(8,128)(2,1)}, u32[]{:S(2)}, u32[]{:S(2)}) collective-permute-start(bf16[512,1024]{1,0:T(8,128)(2,1)S(1)} %pad_maximum_fusion.near_ref), channel_id=1, source_target_pairs={{0,1},{1,0},{2,3},{3,2},{4,5},{5,4},{6,7},{7,6},{8,9},{9,8},{10,11... | collective-permute-start | bytes 3145736 | tf_op jit(solution)/shard_map/ppermute | solution.py:79
  67.9 13.9 %all-to-all-start.2 = ((f32[8,16,192]{2,1,0:T(8,128)}), f32[8,16,192]{2,1,0:T(8,128)S(1)}, u32[]{:S(2)}, u32[]{:S(2)}) async-start(f32[8,16,192]{2,1,0:T(8,128)} %broadcast_in_dim.135), calls=%async_computation.2 | async-start | bytes 262144 | tf_op jit(solution)/shard_map/all_to_all | solution.py:83
  81.8 4.5 %shard_map.102 = bf16[768,1024]{1,0:T(8,128)(2,1)} custom-call(s32[1]{0:T(128)} %bitcast.6.core_ref, bf16[768,1024]{1,0:T(8,128)(2,1)S(1)} %bitcast.51, bf16[512,1024]{1,0:T(8,128)(2,1)S(1)} %pad_maximum_fusion.near_ref, bf16[512,1024]{1,0:T(8,128)(2,1)} %collective-permute-done.7.far_ref), custom_call_target="tpu_custom_call" | custom-call | flops 1610612736 | bytes 5242880 | tf_op jit(solution)/shard_map/pallas_call | solution.py:112
  86.3 4.5 %all-to-all-done.2 = f32[8,16,192]{2,1,0:T(8,128)S(1)} async-done(((f32[8,16,192]{2,1,0:T(8,128)}), f32[8,16,192]{2,1,0:T(8,128)S(1)}, u32[]{:S(2)}, u32[]{:S(2)}) %all-to-all-start.2) | async-done | bytes 98336 | tf_op jit(solution)/shard_map/all_to_all | solution.py:83
  90.9 3.7 %all-to-all-start.3 = ((bf16[8,96,1024]{2,1,0:T(8,128)(2,1)}), bf16[8,96,1024]{2,1,0:T(8,128)(2,1)S(1)}, u32[]{:S(2)}, u32[]{:S(2)}) async-start(bf16[8,96,1024]{2,1,0:T(8,128)(2,1)} %bitcast.19), calls=%async_computation.3 | async-start | bytes 3145728 | tf_op jit(solution)/shard_map/all_to_all | solution.py:83
  94.7 1.9 %collective-permute-start.8 = (bf16[112,256]{1,0:T(8,128)(2,1)S(1)}, bf16[112,256]{1,0:T(8,128)(2,1)S(1)}, u32[]{:S(2)}, u32[]{:S(2)}) collective-permute-start(bf16[112,256]{1,0:T(8,128)(2,1)S(1)} %fusion.11), channel_id=1, source_target_pairs={{0,1},{1,0},{2,3},{3,2},{4,5},{5,4},{6,7},{7,6},{8,9},{9,8},{10,11... | collective-permute-start | bytes 172040 | tf_op jit(solution)/shard_map/ppermute | solution.py:79
  98.3 3.3 %collective-permute-start.9 = (bf16[192,256]{1,0:T(8,128)(2,1)S(1)}, bf16[192,256]{1,0:T(8,128)(2,1)S(1)}, u32[]{:S(2)}, u32[]{:S(2)}) collective-permute-start(bf16[192,256]{1,0:T(8,128)(2,1)S(1)} %bitcast.64), channel_id=1, source_target_pairs={{0,256},{1,257},{2,258},{3,259},{4,260},{5,261},{6,262},{7,263},{8... | collective-permute-start | bytes 294920 | tf_op jit(solution)/shard_map/ppermute | solution.py:79
  101.8 4.7 %collective-permute-done.9 = bf16[192,256]{1,0:T(8,128)(2,1)S(1)} collective-permute-done((bf16[192,256]{1,0:T(8,128)(2,1)S(1)}, bf16[192,256]{1,0:T(8,128)(2,1)S(1)}, u32[]{:S(2)}, u32[]{:S(2)}) %collective-permute-start.9) | collective-permute-done | bytes 98336 | tf_op jit(solution)/shard_map/ppermute | solution.py:79
  108.7 10.4 %all-to-all-done.3 = bf16[8,96,1024]{2,1,0:T(8,128)(2,1)S(1)} async-done(((bf16[8,96,1024]{2,1,0:T(8,128)(2,1)}), bf16[8,96,1024]{2,1,0:T(8,128)(2,1)S(1)}, u32[]{:S(2)}, u32[]{:S(2)}) %all-to-all-start.3) | async-done | bytes 1572896 | tf_op jit(solution)/shard_map/all_to_all | solution.py:83
  121.0 3.2 %collective-permute-start.10 = (bf16[96,512]{1,0:T(8,128)(2,1)S(1)}, bf16[96,512]{1,0:T(8,128)(2,1)S(1)}, u32[]{:S(2)}, u32[]{:S(2)}) collective-permute-start(bf16[96,512]{1,0:T(8,128)(2,1)S(1)} %get-tuple-element.27), channel_id=1, source_target_pairs={{0,0},{1,1},{2,16},{3,3},{4,32},{5,5},{6,48},{7,7},{8,64},{9,9},{1... | collective-permute-start | bytes 294920 | tf_op jit(solution)/shard_map/ppermute | solution.py:79
  124.2 1.9 %collective-permute-start.11 = (bf16[96,512]{1,0:T(8,128)(2,1)S(1)}, bf16[96,512]{1,0:T(8,128)(2,1)S(1)}, u32[]{:S(2)}, u32[]{:S(2)}) collective-permute-start(bf16[96,512]{1,0:T(8,128)(2,1)S(1)} %get-tuple-element.28), channel_id=1, source_target_pairs={{0,16},{1,3},{2,0},{3,1},{4,48},{5,7},{6,32},{7,5},{8,80},{9,11},{... | collective-permute-start | bytes 294920 | tf_op jit(solution)/shard_map/ppermute | solution.py:79
  126.2 8.1 %all-to-all-start.4 = ((bf16[8,128,256]{2,1,0:T(8,128)(2,1)}), bf16[8,128,256]{2,1,0:T(8,128)(2,1)S(1)}, u32[]{:S(2)}, u32[]{:S(2)}) async-start(bf16[8,128,256]{2,1,0:T(8,128)(2,1)} %reshape.347), calls=%async_computation.4 | async-start | bytes 1048576 | tf_op jit(solution)/shard_map/all_to_all | solution.py:83
  136.1 1.9 %collective-permute-start.12 = (bf16[192,256]{1,0:T(8,128)(2,1)S(1)}, bf16[192,256]{1,0:T(8,128)(2,1)S(1)}, u32[]{:S(2)}, u32[]{:S(2)}) collective-permute-start(bf16[192,256]{1,0:T(8,128)(2,1)S(1)} %pad_maximum_fusion.3), channel_id=1, source_target_pairs={{0,1},{1,0},{2,3},{3,2},{4,5},{5,4},{6,7},{7,6},{8,9},{9,8},{10,11... | collective-permute-start | bytes 294920 | tf_op jit(solution)/shard_map/ppermute | solution.py:79
  141.0 5.8 %all-to-all-done.4 = bf16[8,128,256]{2,1,0:T(8,128)(2,1)S(1)} async-done(((bf16[8,128,256]{2,1,0:T(8,128)(2,1)}), bf16[8,128,256]{2,1,0:T(8,128)(2,1)S(1)}, u32[]{:S(2)}, u32[]{:S(2)}) %all-to-all-start.4) | async-done | bytes 524320 | tf_op jit(solution)/shard_map/all_to_all | solution.py:83
  (95 shorter events, 24.8 us)
Async XLA Ops:
  1.7 6.2 %collective-permute-start = (bf16[256,256]{1,0:T(8,128)(2,1)S(1)}, bf16[256,256]{1,0:T(8,128)(2,1)S(1)}, u32[]{:S(2)}, u32[]{:S(2)}) collective-permute-start(bf16[256,256]{1,0:T(8,128)(2,1)S(1)} %get-tuple-element.35), channel_id=1, source_target_pairs={{0,1},{1,0},{2,3},{3,2},{4,5},{5,4},{6,7},{7,6},{8,9},{9,8},{10,11... | collective-permute-start | bytes 393224 | tf_op jit(solution)/shard_map/ppermute | solution.py:79
  3.6 16.4 %collective-permute-start.3 = (bf16[256,512]{1,0:T(8,128)(2,1)}, bf16[256,512]{1,0:T(8,128)(2,1)S(1)}, u32[]{:S(2)}, u32[]{:S(2)}) collective-permute-start(bf16[256,512]{1,0:T(8,128)(2,1)} %param.8), channel_id=1, source_target_pairs={{0,2},{1,3},{2,0},{3,1},{4,6},{5,7},{6,4},{7,5},{8,10},{9,11},{10,... | collective-permute-start | bytes 786440 | tf_op jit(solution)/shard_map/ppermute | solution.py:79
  7.9 12.1 %copy-start = (bf16[256,512]{1,0:T(8,128)(2,1)S(1)}, bf16[256,512]{1,0:T(8,128)(2,1)}, u32[]{:S(2)}) copy-start(bf16[256,512]{1,0:T(8,128)(2,1)} %param.8) | copy-start | bytes 786436
  8.1 11.8 %collective-permute-start.2 = (bf16[96,512]{1,0:T(8,128)(2,1)S(1)}, bf16[96,512]{1,0:T(8,128)(2,1)S(1)}, u32[]{:S(2)}, u32[]{:S(2)}) collective-permute-start(bf16[96,512]{1,0:T(8,128)(2,1)S(1)} %get-tuple-element.43), channel_id=1, source_target_pairs={{0,2},{1,3},{2,0},{3,35},{4,6},{5,67},{6,4},{7,99},{8,10},{9,131},... | collective-permute-start | bytes 294920 | tf_op jit(solution)/shard_map/ppermute | solution.py:79
  11.3 12.9 %collective-permute-start.1 = (bf16[96,512]{1,0:T(8,128)(2,1)S(1)}, bf16[96,512]{1,0:T(8,128)(2,1)S(1)}, u32[]{:S(2)}, u32[]{:S(2)}) collective-permute-start(bf16[96,512]{1,0:T(8,128)(2,1)S(1)} %get-tuple-element.42), channel_id=1, source_target_pairs={{0,0},{1,1},{2,2},{3,33},{4,4},{5,65},{6,6},{7,97},{8,8},{9,129},{... | collective-permute-start | bytes 294920 | tf_op jit(solution)/shard_map/ppermute | solution.py:79
  12.8 20.7 %all-to-all-start = ((bf16[8,64,512]{2,1,0:T(8,128)(2,1)}), bf16[8,64,512]{2,1,0:T(8,128)(2,1)S(1)}, u32[]{:S(2)}, u32[]{:S(2)}) async-start(bf16[8,64,512]{2,1,0:T(8,128)(2,1)} %broadcast_in_dim.122), calls=%async_computation | async-start | bytes 1048576 | tf_op jit(solution)/shard_map/all_to_all | solution.py:83
  20.2 12.7 %collective-permute-start.4 = (bf16[520,512]{1,0:T(8,128)(2,1)S(1)}, bf16[520,512]{1,0:T(8,128)(2,1)S(1)}, u32[]{:S(2)}, u32[]{:S(2)}) collective-permute-start(bf16[520,512]{1,0:T(8,128)(2,1)S(1)} %maximum_maximum_fusion), channel_id=1, source_target_pairs={{0,256},{1,257},{2,258},{3,259},{4,260},{5,261},{6,262},{7,263},{8... | collective-permute-start | bytes 1597448 | tf_op jit(solution)/shard_map/ppermute | solution.py:79
  34.9 7.8 %copy-start.3 = (s32[1,6]{1,0:T(1,128)S(1)}, s32[1,6]{1,0:T(1,128)}, u32[]{:S(2)}) copy-start(s32[1,6]{1,0:T(1,128)} %param.11) | copy-start | bytes 76
  34.9 32.3 %all-to-all-start.1 = ((bf16[8,96,1024]{2,1,0:T(8,128)(2,1)}), bf16[8,96,1024]{2,1,0:T(8,128)(2,1)S(1)}, u32[]{:S(2)}, u32[]{:S(2)}) async-start(bf16[8,96,1024]{2,1,0:T(8,128)(2,1)} %broadcast_in_dim.124), calls=%async_computation.1 | async-start | bytes 3145728 | tf_op jit(solution)/shard_map/all_to_all | solution.py:83
  43.6 8.1 %collective-permute-start.5 = (bf16[96,512]{1,0:T(8,128)(2,1)S(1)}, bf16[96,512]{1,0:T(8,128)(2,1)}, u32[]{:S(2)}, u32[]{:S(2)}) collective-permute-start(bf16[96,512]{1,0:T(8,128)(2,1)S(1)} %bitcast_select_fusion.2), channel_id=1, source_target_pairs={{0,256},{1,257},{2,258},{3,259},{4,260},{5,261},{6,262},{7,263},{8... | collective-permute-start | bytes 294920 | tf_op jit(solution)/shard_map/ppermute | solution.py:79
  52.9 8.6 %collective-permute-start.6 = (f32[16,192]{1,0:T(8,128)S(1)}, f32[16,192]{1,0:T(8,128)S(1)}, u32[]{:S(2)}, u32[]{:S(2)}) collective-permute-start(f32[16,192]{1,0:T(8,128)S(1)} %fusion.1), channel_id=1, source_target_pairs={{0,2},{1,3},{2,0},{3,1},{4,6},{5,7},{6,4},{7,5},{8,10},{9,11},{10,... | collective-permute-start | bytes 36872 | tf_op jit(solution)/shard_map/ppermute | solution.py:79
  61.6 20.2 %collective-permute-start.7 = (bf16[512,1024]{1,0:T(8,128)(2,1)S(1)}, bf16[512,1024]{1,0:T(8,128)(2,1)}, u32[]{:S(2)}, u32[]{:S(2)}) collective-permute-start(bf16[512,1024]{1,0:T(8,128)(2,1)S(1)} %pad_maximum_fusion.near_ref), channel_id=1, source_target_pairs={{0,1},{1,0},{2,3},{3,2},{4,5},{5,4},{6,7},{7,6},{8,9},{9,8},{10,11... | collective-permute-start | bytes 3145736 | tf_op jit(solution)/shard_map/ppermute | solution.py:79
  67.9 23.0 %all-to-all-start.2 = ((f32[8,16,192]{2,1,0:T(8,128)}), f32[8,16,192]{2,1,0:T(8,128)S(1)}, u32[]{:S(2)}, u32[]{:S(2)}) async-start(f32[8,16,192]{2,1,0:T(8,128)} %broadcast_in_dim.135), calls=%async_computation.2 | async-start | bytes 262144 | tf_op jit(solution)/shard_map/all_to_all | solution.py:83
  90.8 7.0 %copy-start.1 = (bf16[192,256]{1,0:T(8,128)(2,1)S(1)}, bf16[192,256]{1,0:T(8,128)(2,1)}, u32[]{:S(2)}) copy-start(bf16[192,256]{1,0:T(8,128)(2,1)} %param.7) | copy-start | bytes 294916
  90.9 7.1 %copy-start.2 = (bf16[192,256]{1,0:T(8,128)(2,1)S(1)}, bf16[192,256]{1,0:T(8,128)(2,1)}, u32[]{:S(2)}) copy-start(bf16[192,256]{1,0:T(8,128)(2,1)} %param.13) | copy-start | bytes 294916
  90.9 7.1 %copy-start.6 = (bf16[192]{0:T(256)(128)(2,1)S(1)}, bf16[192]{0:T(256)(128)(2,1)}, u32[]{:S(2)}) copy-start(bf16[192]{0:T(256)(128)(2,1)} %copy-done.5) | copy-start | bytes 1156
  90.9 10.7 %copy-start.4 = (s32[1,6]{1,0:T(1,128)S(1)}, s32[1,6]{1,0:T(1,128)}, u32[]{:S(2)}) copy-start(s32[1,6]{1,0:T(1,128)} %param.11) | copy-start | bytes 76
  90.9 28.2 %all-to-all-start.3 = ((bf16[8,96,1024]{2,1,0:T(8,128)(2,1)}), bf16[8,96,1024]{2,1,0:T(8,128)(2,1)S(1)}, u32[]{:S(2)}, u32[]{:S(2)}) async-start(bf16[8,96,1024]{2,1,0:T(8,128)(2,1)} %bitcast.19), calls=%async_computation.3 | async-start | bytes 3145728 | tf_op jit(solution)/shard_map/all_to_all | solution.py:83
  94.7 3.1 %collective-permute-start.8 = (bf16[112,256]{1,0:T(8,128)(2,1)S(1)}, bf16[112,256]{1,0:T(8,128)(2,1)S(1)}, u32[]{:S(2)}, u32[]{:S(2)}) collective-permute-start(bf16[112,256]{1,0:T(8,128)(2,1)S(1)} %fusion.11), channel_id=1, source_target_pairs={{0,1},{1,0},{2,3},{3,2},{4,5},{5,4},{6,7},{7,6},{8,9},{9,8},{10,11... | collective-permute-start | bytes 172040 | tf_op jit(solution)/shard_map/ppermute | solution.py:79
  98.3 8.3 %collective-permute-start.9 = (bf16[192,256]{1,0:T(8,128)(2,1)S(1)}, bf16[192,256]{1,0:T(8,128)(2,1)S(1)}, u32[]{:S(2)}, u32[]{:S(2)}) collective-permute-start(bf16[192,256]{1,0:T(8,128)(2,1)S(1)} %bitcast.64), channel_id=1, source_target_pairs={{0,256},{1,257},{2,258},{3,259},{4,260},{5,261},{6,262},{7,263},{8... | collective-permute-start | bytes 294920 | tf_op jit(solution)/shard_map/ppermute | solution.py:79
  121.0 13.2 %collective-permute-start.10 = (bf16[96,512]{1,0:T(8,128)(2,1)S(1)}, bf16[96,512]{1,0:T(8,128)(2,1)S(1)}, u32[]{:S(2)}, u32[]{:S(2)}) collective-permute-start(bf16[96,512]{1,0:T(8,128)(2,1)S(1)} %get-tuple-element.27), channel_id=1, source_target_pairs={{0,0},{1,1},{2,16},{3,3},{4,32},{5,5},{6,48},{7,7},{8,64},{9,9},{1... | collective-permute-start | bytes 294920 | tf_op jit(solution)/shard_map/ppermute | solution.py:79
  124.2 11.9 %collective-permute-start.11 = (bf16[96,512]{1,0:T(8,128)(2,1)S(1)}, bf16[96,512]{1,0:T(8,128)(2,1)S(1)}, u32[]{:S(2)}, u32[]{:S(2)}) collective-permute-start(bf16[96,512]{1,0:T(8,128)(2,1)S(1)} %get-tuple-element.28), channel_id=1, source_target_pairs={{0,16},{1,3},{2,0},{3,1},{4,48},{5,7},{6,32},{7,5},{8,80},{9,11},{... | collective-permute-start | bytes 294920 | tf_op jit(solution)/shard_map/ppermute | solution.py:79
  126.2 20.7 %all-to-all-start.4 = ((bf16[8,128,256]{2,1,0:T(8,128)(2,1)}), bf16[8,128,256]{2,1,0:T(8,128)(2,1)S(1)}, u32[]{:S(2)}, u32[]{:S(2)}) async-start(bf16[8,128,256]{2,1,0:T(8,128)(2,1)} %reshape.347), calls=%async_computation.4 | async-start | bytes 1048576 | tf_op jit(solution)/shard_map/all_to_all | solution.py:83
  136.1 3.2 %collective-permute-start.12 = (bf16[192,256]{1,0:T(8,128)(2,1)S(1)}, bf16[192,256]{1,0:T(8,128)(2,1)S(1)}, u32[]{:S(2)}, u32[]{:S(2)}) collective-permute-start(bf16[192,256]{1,0:T(8,128)(2,1)S(1)} %pad_maximum_fusion.3), channel_id=1, source_target_pairs={{0,1},{1,0},{2,3},{3,2},{4,5},{5,4},{6,7},{7,6},{8,9},{9,8},{10,11... | collective-permute-start | bytes 294920 | tf_op jit(solution)/shard_map/ppermute | solution.py:79
  (1 other events, 0.7 us)

commit v4 on v3

--- a/solution.py
+++ b/solution.py
@@ -156,17 +156,19 @@
         permute(jnp.where(side == 0, top, bottom), TO_BLOCKS[0]),
         permute(jnp.where(side == 0, bottom, top), TO_BLOCKS[1]),
     ]
+    near_rows = permute(output_weight, SWAP_LOW)
+    got[0], near_rows, slots = together((got[0], near_rows, slots))
     flip = (xh ^ xl) == 1
     rows_x = jnp.concatenate([got[0][:, :width], got[1][:, :width], got[0][:, width:], got[1][:, width:]], 1)
     rows_g = jnp.concatenate([jnp.where(flip, got[1], got[0]), jnp.where(flip, got[0], got[1])], 1)
     rows = jnp.where(first, rows_x, rows_g)
-    block = jnp.concatenate([output_weight, permute(output_weight, SWAP_LOW)], 0)
+    block = jnp.concatenate([output_weight, near_rows], 0)
     numbers = jnp.pad(slots.astype(BF16), (0, 8 - SLOTS))
     numbers = jnp.broadcast_to(numbers[:, None], (8, block.shape[1]))
     came = permute(jnp.concatenate([block, numbers], 0), SWAP_HIGH)
+    other_slots = came[-8:, 0][:SLOTS].astype(jnp.int32)
+    rows, block, tables = together((rows, block, tables))
     near = jnp.concatenate([block, came[:-8]], 1)
-    other_slots = came[-8:, 0][:SLOTS].astype(jnp.int32)
-    rows, near, tables, other_slots = together((rows, near, tables, other_slots))
     gathered = exchange(jnp.broadcast_to(rows[None], (RING,) + rows.shape), GROUPS_GATHER)
 
     def pick(which):

time: 149 us -> 146 us (0.980)
  waiting for transfers between devices: 44.9 us -> 39.5 us
  local copies, waits for them, and re-layouts: 8.72 us -> 10.5 us
    ppermute x13, waiting for transfers between devices: 23.1 us -> 11.6 us  [permute(): return lax.ppermute(value, AXES, where)]
    ppermute x13, starting transfers between devices: 39.4 us -> 45.5 us  [permute(): return lax.ppermute(value, AXES, where)]
    all_to_all x5, waiting for transfers between devices: 21.9 us -> 27.8 us  [exchange(): lax.all_to_all(value, AXES, 0, 0, axis_index_groups=groups, tiled=True)]
    all_to_all x5, starting transfers between devices: 40.6 us -> 35.3 us  [exchange(): lax.all_to_all(value, AXES, 0, 0, axis_index_groups=groups, tiled=True)]
    slice x1, local copies, waits for them, and re-layouts: 0.03 us -> 1.88 us  [body(): near = jnp.concatenate([block, came[:-8]], 1)]
  transfers between devices with their start and end apart: 18 -> 18, of which waited for: 12 -> 11; matrix products, arithmetic and copies ran while one was open for 8% -> 10% of each run, Pallas kernels for 3% -> 3%
where the time goes in v4:
time: 146 us; the launch traced here: 144 us
  starting transfers between devices  80.8 us (55%)
  waiting for transfers between devices  39.5 us (27%)
  local copies, waits for them, and re-layouts  10.5 us (7%)
  other arithmetic  5.1 us (3%)
  Pallas kernels  4.55 us (3%)
  matrix products  2.62 us (2%)
    ppermute x13, starting transfers between devices, permute(): return lax.ppermute(value, AXES, where)  45.5 us
    all_to_all x5, starting transfers between devices, exchange(): lax.all_to_all(value, AXES, 0, 0, axis_index_groups=groups, tiled=True)  35.3 us
    all_to_all x5, waiting for transfers between devices, exchange(): lax.all_to_all(value, AXES, 0, 0, axis_index_groups=groups, tiled=True)  27.8 us
    ppermute x13, waiting for transfers between devices, permute(): return lax.ppermute(value, AXES, where)  11.6 us
    pallas_call x1, Pallas kernels, product(): pl.pallas_call(product_kernel, grid=(count // tile,), in_specs=[pl.BlockS...  4.55 us
  transfers between devices with their start and end apart: 18, of which 11 were waited for; matrix products, arithmetic and copies ran while one was open for 10% of the time, Pallas kernels for 3%

profile of v4, /device:TPU:6, one launch (start us, length us, event | category | flops | bytes accessed | tf_op | source)
XLA Modules:
  0.0 144.3 jit_solution(737442158086964349)
XLA Ops:
  1.7 1.9 %collective-permute-start = (bf16[256,256]{1,0:T(8,128)(2,1)S(1)}, bf16[256,256]{1,0:T(8,128)(2,1)S(1)}, u32[]{:S(2)}, u32[]{:S(2)}) collective-permute-start(bf16[256,256]{1,0:T(8,128)(2,1)S(1)} %get-tuple-element.41), channel_id=1, source_target_pairs={{0,1},{1,0},{2,3},{3,2},{4,5},{5,4},{6,7},{7,6},{8,9},{9,8},{10,11... | collective-permute-start | bytes 393224 | tf_op jit(solution)/shard_map/ppermute | solution.py:79
  5.2 2.7 %collective-permute-start.4 = (bf16[96,512]{1,0:T(8,128)(2,1)S(1)}, bf16[96,512]{1,0:T(8,128)(2,1)S(1)}, u32[]{:S(2)}, u32[]{:S(2)}) collective-permute-start(bf16[96,512]{1,0:T(8,128)(2,1)S(1)} %get-tuple-element.49), channel_id=1, source_target_pairs={{0,2},{1,3},{2,0},{3,35},{4,6},{5,67},{6,4},{7,99},{8,10},{9,131},... | collective-permute-start | bytes 294920 | tf_op jit(solution)/shard_map/ppermute | solution.py:79
  8.0 3.1 %collective-permute-start.2 = (bf16[256,512]{1,0:T(8,128)(2,1)S(1)}, bf16[256,512]{1,0:T(8,128)(2,1)S(1)}, u32[]{:S(2)}, u32[]{:S(2)}) collective-permute-start(bf16[256,512]{1,0:T(8,128)(2,1)S(1)} %copy-done), channel_id=1, source_target_pairs={{0,2},{1,3},{2,0},{3,1},{4,6},{5,7},{6,4},{7,5},{8,10},{9,11},{10,... | collective-permute-start | bytes 786440 | tf_op jit(solution)/shard_map/ppermute | solution.py:79
  12.6 7.1 %all-to-all-start = ((bf16[8,64,512]{2,1,0:T(8,128)(2,1)}), bf16[8,64,512]{2,1,0:T(8,128)(2,1)S(1)}, u32[]{:S(2)}, u32[]{:S(2)}) async-start(bf16[8,64,512]{2,1,0:T(8,128)(2,1)} %broadcast_in_dim.124), calls=%async_computation | async-start | bytes 1048576 | tf_op jit(solution)/shard_map/all_to_all | solution.py:83
  20.0 5.3 %collective-permute-start.3 = (bf16[520,512]{1,0:T(8,128)(2,1)S(1)}, bf16[520,512]{1,0:T(8,128)(2,1)}, u32[]{:S(2)}, u32[]{:S(2)}) collective-permute-start(bf16[520,512]{1,0:T(8,128)(2,1)S(1)} %maximum_maximum_fusion), channel_id=1, source_target_pairs={{0,256},{1,257},{2,258},{3,259},{4,260},{5,261},{6,262},{7,263},{8... | collective-permute-start | bytes 1597448 | tf_op jit(solution)/shard_map/ppermute | solution.py:79
  25.4 7.0 %all-to-all-done = bf16[8,64,512]{2,1,0:T(8,128)(2,1)S(1)} async-done(((bf16[8,64,512]{2,1,0:T(8,128)(2,1)}), bf16[8,64,512]{2,1,0:T(8,128)(2,1)S(1)}, u32[]{:S(2)}, u32[]{:S(2)}) %all-to-all-start) | async-done | bytes 524320 | tf_op jit(solution)/shard_map/all_to_all | solution.py:83
  33.8 4.7 %all-to-all-start.1 = ((bf16[8,96,1024]{2,1,0:T(8,128)(2,1)}), bf16[8,96,1024]{2,1,0:T(8,128)(2,1)S(1)}, u32[]{:S(2)}, u32[]{:S(2)}) async-start(bf16[8,96,1024]{2,1,0:T(8,128)(2,1)} %broadcast_in_dim.125), calls=%async_computation.1 | async-start | bytes 3145728 | tf_op jit(solution)/shard_map/all_to_all | solution.py:83
  40.2 3.6 %collective-permute-start.5 = (bf16[96,512]{1,0:T(8,128)(2,1)S(1)}, bf16[96,512]{1,0:T(8,128)(2,1)S(1)}, u32[]{:S(2)}, u32[]{:S(2)}) collective-permute-start(bf16[96,512]{1,0:T(8,128)(2,1)S(1)} %bitcast_select_fusion.2), channel_id=1, source_target_pairs={{0,256},{1,257},{2,258},{3,259},{4,260},{5,261},{6,262},{7,263},{8... | collective-permute-start | bytes 294920 | tf_op jit(solution)/shard_map/ppermute | solution.py:79
  44.0 1.9 %slice.106 = bf16[512,512]{1,0:T(8,128)(2,1)} slice(bf16[520,512]{1,0:T(8,128)(2,1)} %collective-permute-done.3), slice={[0:512], [0:512]} | slice | bytes 1048576 | tf_op jit(solution)/shard_map/slice | solution.py:171
  48.5 6.4 %collective-permute-start.6 = (f32[16,192]{1,0:T(8,128)S(1)}, f32[16,192]{1,0:T(8,128)S(1)}, u32[]{:S(2)}, u32[]{:S(2)}) collective-permute-start(f32[16,192]{1,0:T(8,128)S(1)} %fusion.1), channel_id=1, source_target_pairs={{0,2},{1,3},{2,0},{3,1},{4,6},{5,7},{6,4},{7,5},{8,10},{9,11},{10,... | collective-permute-start | bytes 36872 | tf_op jit(solution)/shard_map/ppermute | solution.py:79
  56.6 10.0 %collective-permute-start.7 = (bf16[512,1024]{1,0:T(8,128)(2,1)S(1)}, bf16[512,1024]{1,0:T(8,128)(2,1)}, u32[]{:S(2)}, u32[]{:S(2)}) collective-permute-start(bf16[512,1024]{1,0:T(8,128)(2,1)S(1)} %pad_maximum_fusion.near_ref), channel_id=1, source_target_pairs={{0,1},{1,0},{2,3},{3,2},{4,5},{5,4},{6,7},{7,6},{8,9},{9,8},{10,11... | collective-permute-start | bytes 3145736 | tf_op jit(solution)/shard_map/ppermute | solution.py:79
  67.3 11.7 %all-to-all-start.2 = ((f32[8,16,192]{2,1,0:T(8,128)}), f32[8,16,192]{2,1,0:T(8,128)S(1)}, u32[]{:S(2)}, u32[]{:S(2)}) async-start(f32[8,16,192]{2,1,0:T(8,128)} %broadcast_in_dim.136), calls=%async_computation.2 | async-start | bytes 262144 | tf_op jit(solution)/shard_map/all_to_all | solution.py:83
  79.0 4.6 %shard_map.102 = bf16[768,1024]{1,0:T(8,128)(2,1)} custom-call(s32[1]{0:T(128)} %bitcast.5.core_ref, bf16[768,1024]{1,0:T(8,128)(2,1)S(1)} %bitcast.43, bf16[512,1024]{1,0:T(8,128)(2,1)S(1)} %pad_maximum_fusion.near_ref, bf16[512,1024]{1,0:T(8,128)(2,1)} %collective-permute-done.7.far_ref), custom_call_target="tpu_custom_call" | custom-call | flops 1610612736 | bytes 5242880 | tf_op jit(solution)/shard_map/pallas_call | solution.py:112
  83.6 4.5 %all-to-all-done.2 = f32[8,16,192]{2,1,0:T(8,128)S(1)} async-done(((f32[8,16,192]{2,1,0:T(8,128)}), f32[8,16,192]{2,1,0:T(8,128)S(1)}, u32[]{:S(2)}, u32[]{:S(2)}) %all-to-all-start.2) | async-done | bytes 98336 | tf_op jit(solution)/shard_map/all_to_all | solution.py:83
  88.1 3.7 %all-to-all-start.3 = ((bf16[8,96,1024]{2,1,0:T(8,128)(2,1)}), bf16[8,96,1024]{2,1,0:T(8,128)(2,1)S(1)}, u32[]{:S(2)}, u32[]{:S(2)}) async-start(bf16[8,96,1024]{2,1,0:T(8,128)(2,1)} %bitcast.17), calls=%async_computation.3 | async-start | bytes 3145728 | tf_op jit(solution)/shard_map/all_to_all | solution.py:83
  91.9 1.9 %collective-permute-start.8 = (bf16[112,256]{1,0:T(8,128)(2,1)S(1)}, bf16[112,256]{1,0:T(8,128)(2,1)S(1)}, u32[]{:S(2)}, u32[]{:S(2)}) collective-permute-start(bf16[112,256]{1,0:T(8,128)(2,1)S(1)} %fusion.11), channel_id=1, source_target_pairs={{0,1},{1,0},{2,3},{3,2},{4,5},{5,4},{6,7},{7,6},{8,9},{9,8},{10,11... | collective-permute-start | bytes 172040 | tf_op jit(solution)/shard_map/ppermute | solution.py:79
  95.5 3.3 %collective-permute-start.9 = (bf16[192,256]{1,0:T(8,128)(2,1)S(1)}, bf16[192,256]{1,0:T(8,128)(2,1)S(1)}, u32[]{:S(2)}, u32[]{:S(2)}) collective-permute-start(bf16[192,256]{1,0:T(8,128)(2,1)S(1)} %bitcast.56), channel_id=1, source_target_pairs={{0,256},{1,257},{2,258},{3,259},{4,260},{5,261},{6,262},{7,263},{8... | collective-permute-start | bytes 294920 | tf_op jit(solution)/shard_map/ppermute | solution.py:79
  99.1 4.7 %collective-permute-done.9 = bf16[192,256]{1,0:T(8,128)(2,1)S(1)} collective-permute-done((bf16[192,256]{1,0:T(8,128)(2,1)S(1)}, bf16[192,256]{1,0:T(8,128)(2,1)S(1)}, u32[]{:S(2)}, u32[]{:S(2)}) %collective-permute-start.9) | collective-permute-done | bytes 98336 | tf_op jit(solution)/shard_map/ppermute | solution.py:79
  105.9 10.4 %all-to-all-done.3 = bf16[8,96,1024]{2,1,0:T(8,128)(2,1)S(1)} async-done(((bf16[8,96,1024]{2,1,0:T(8,128)(2,1)}), bf16[8,96,1024]{2,1,0:T(8,128)(2,1)S(1)}, u32[]{:S(2)}, u32[]{:S(2)}) %all-to-all-start.3) | async-done | bytes 1572896 | tf_op jit(solution)/shard_map/all_to_all | solution.py:83
  118.2 2.8 %collective-permute-start.10 = (bf16[96,512]{1,0:T(8,128)(2,1)S(1)}, bf16[96,512]{1,0:T(8,128)(2,1)S(1)}, u32[]{:S(2)}, u32[]{:S(2)}) collective-permute-start(bf16[96,512]{1,0:T(8,128)(2,1)S(1)} %get-tuple-element.31), channel_id=1, source_target_pairs={{0,0},{1,1},{2,16},{3,3},{4,32},{5,5},{6,48},{7,7},{8,64},{9,9},{1... | collective-permute-start | bytes 294920 | tf_op jit(solution)/shard_map/ppermute | solution.py:79
  121.0 1.9 %collective-permute-start.11 = (bf16[96,512]{1,0:T(8,128)(2,1)S(1)}, bf16[96,512]{1,0:T(8,128)(2,1)S(1)}, u32[]{:S(2)}, u32[]{:S(2)}) collective-permute-start(bf16[96,512]{1,0:T(8,128)(2,1)S(1)} %get-tuple-element.32), channel_id=1, source_target_pairs={{0,16},{1,3},{2,0},{3,1},{4,48},{5,7},{6,32},{7,5},{8,80},{9,11},{... | collective-permute-start | bytes 294920 | tf_op jit(solution)/shard_map/ppermute | solution.py:79
  122.9 8.1 %all-to-all-start.4 = ((bf16[8,128,256]{2,1,0:T(8,128)(2,1)}), bf16[8,128,256]{2,1,0:T(8,128)(2,1)S(1)}, u32[]{:S(2)}, u32[]{:S(2)}) async-start(bf16[8,128,256]{2,1,0:T(8,128)(2,1)} %reshape.200), calls=%async_computation.4 | async-start | bytes 1048576 | tf_op jit(solution)/shard_map/all_to_all | solution.py:83
  132.8 1.9 %collective-permute-start.12 = (bf16[192,256]{1,0:T(8,128)(2,1)S(1)}, bf16[192,256]{1,0:T(8,128)(2,1)S(1)}, u32[]{:S(2)}, u32[]{:S(2)}) collective-permute-start(bf16[192,256]{1,0:T(8,128)(2,1)S(1)} %pad_maximum_fusion.4), channel_id=1, source_target_pairs={{0,1},{1,0},{2,3},{3,2},{4,5},{5,4},{6,7},{7,6},{8,9},{9,8},{10,11... | collective-permute-start | bytes 294920 | tf_op jit(solution)/shard_map/ppermute | solution.py:79
  137.7 5.9 %all-to-all-done.4 = bf16[8,128,256]{2,1,0:T(8,128)(2,1)S(1)} async-done(((bf16[8,128,256]{2,1,0:T(8,128)(2,1)}), bf16[8,128,256]{2,1,0:T(8,128)(2,1)S(1)}, u32[]{:S(2)}, u32[]{:S(2)}) %all-to-all-start.4) | async-done | bytes 524320 | tf_op jit(solution)/shard_map/all_to_all | solution.py:83
  (88 shorter events, 24.0 us)
Async XLA Ops:
  0.6 7.3 %copy-start = (bf16[256,512]{1,0:T(8,128)(2,1)S(1)}, bf16[256,512]{1,0:T(8,128)(2,1)}, u32[]{:S(2)}) copy-start(bf16[256,512]{1,0:T(8,128)(2,1)} %param.8) | copy-start | bytes 786436
  1.7 3.2 %collective-permute-start = (bf16[256,256]{1,0:T(8,128)(2,1)S(1)}, bf16[256,256]{1,0:T(8,128)(2,1)S(1)}, u32[]{:S(2)}, u32[]{:S(2)}) collective-permute-start(bf16[256,256]{1,0:T(8,128)(2,1)S(1)} %get-tuple-element.41), channel_id=1, source_target_pairs={{0,1},{1,0},{2,3},{3,2},{4,5},{5,4},{6,7},{7,6},{8,9},{9,8},{10,11... | collective-permute-start | bytes 393224 | tf_op jit(solution)/shard_map/ppermute | solution.py:79
  5.0 14.8 %copy-start.3 = (s32[1,6]{1,0:T(1,128)S(1)}, s32[1,6]{1,0:T(1,128)}, u32[]{:S(2)}) copy-start(s32[1,6]{1,0:T(1,128)} %param.11) | copy-start | bytes 76
  5.2 14.5 %collective-permute-start.4 = (bf16[96,512]{1,0:T(8,128)(2,1)S(1)}, bf16[96,512]{1,0:T(8,128)(2,1)S(1)}, u32[]{:S(2)}, u32[]{:S(2)}) collective-permute-start(bf16[96,512]{1,0:T(8,128)(2,1)S(1)} %get-tuple-element.49), channel_id=1, source_target_pairs={{0,2},{1,3},{2,0},{3,35},{4,6},{5,67},{6,4},{7,99},{8,10},{9,131},... | collective-permute-start | bytes 294920 | tf_op jit(solution)/shard_map/ppermute | solution.py:79
  8.0 11.8 %collective-permute-start.2 = (bf16[256,512]{1,0:T(8,128)(2,1)S(1)}, bf16[256,512]{1,0:T(8,128)(2,1)S(1)}, u32[]{:S(2)}, u32[]{:S(2)}) collective-permute-start(bf16[256,512]{1,0:T(8,128)(2,1)S(1)} %copy-done), channel_id=1, source_target_pairs={{0,2},{1,3},{2,0},{3,1},{4,6},{5,7},{6,4},{7,5},{8,10},{9,11},{10,... | collective-permute-start | bytes 786440 | tf_op jit(solution)/shard_map/ppermute | solution.py:79
  11.1 8.7 %collective-permute-start.1 = (bf16[96,512]{1,0:T(8,128)(2,1)S(1)}, bf16[96,512]{1,0:T(8,128)(2,1)S(1)}, u32[]{:S(2)}, u32[]{:S(2)}) collective-permute-start(bf16[96,512]{1,0:T(8,128)(2,1)S(1)} %get-tuple-element.48), channel_id=1, source_target_pairs={{0,0},{1,1},{2,2},{3,33},{4,4},{5,65},{6,6},{7,97},{8,8},{9,129},{... | collective-permute-start | bytes 294920 | tf_op jit(solution)/shard_map/ppermute | solution.py:79
  12.6 19.8 %all-to-all-start = ((bf16[8,64,512]{2,1,0:T(8,128)(2,1)}), bf16[8,64,512]{2,1,0:T(8,128)(2,1)S(1)}, u32[]{:S(2)}, u32[]{:S(2)}) async-start(bf16[8,64,512]{2,1,0:T(8,128)(2,1)} %broadcast_in_dim.124), calls=%async_computation | async-start | bytes 1048576 | tf_op jit(solution)/shard_map/all_to_all | solution.py:83
  20.0 18.5 %collective-permute-start.3 = (bf16[520,512]{1,0:T(8,128)(2,1)S(1)}, bf16[520,512]{1,0:T(8,128)(2,1)}, u32[]{:S(2)}, u32[]{:S(2)}) collective-permute-start(bf16[520,512]{1,0:T(8,128)(2,1)S(1)} %maximum_maximum_fusion), channel_id=1, source_target_pairs={{0,256},{1,257},{2,258},{3,259},{4,260},{5,261},{6,262},{7,263},{8... | collective-permute-start | bytes 1597448 | tf_op jit(solution)/shard_map/ppermute | solution.py:79
  33.8 32.8 %all-to-all-start.1 = ((bf16[8,96,1024]{2,1,0:T(8,128)(2,1)}), bf16[8,96,1024]{2,1,0:T(8,128)(2,1)S(1)}, u32[]{:S(2)}, u32[]{:S(2)}) async-start(bf16[8,96,1024]{2,1,0:T(8,128)(2,1)} %broadcast_in_dim.125), calls=%async_computation.1 | async-start | bytes 3145728 | tf_op jit(solution)/shard_map/all_to_all | solution.py:83
  40.2 8.0 %collective-permute-start.5 = (bf16[96,512]{1,0:T(8,128)(2,1)S(1)}, bf16[96,512]{1,0:T(8,128)(2,1)S(1)}, u32[]{:S(2)}, u32[]{:S(2)}) collective-permute-start(bf16[96,512]{1,0:T(8,128)(2,1)S(1)} %bitcast_select_fusion.2), channel_id=1, source_target_pairs={{0,256},{1,257},{2,258},{3,259},{4,260},{5,261},{6,262},{7,263},{8... | collective-permute-start | bytes 294920 | tf_op jit(solution)/shard_map/ppermute | solution.py:79
  48.5 8.1 %collective-permute-start.6 = (f32[16,192]{1,0:T(8,128)S(1)}, f32[16,192]{1,0:T(8,128)S(1)}, u32[]{:S(2)}, u32[]{:S(2)}) collective-permute-start(f32[16,192]{1,0:T(8,128)S(1)} %fusion.1), channel_id=1, source_target_pairs={{0,2},{1,3},{2,0},{3,1},{4,6},{5,7},{6,4},{7,5},{8,10},{9,11},{10,... | collective-permute-start | bytes 36872 | tf_op jit(solution)/shard_map/ppermute | solution.py:79
  56.6 22.4 %collective-permute-start.7 = (bf16[512,1024]{1,0:T(8,128)(2,1)S(1)}, bf16[512,1024]{1,0:T(8,128)(2,1)}, u32[]{:S(2)}, u32[]{:S(2)}) collective-permute-start(bf16[512,1024]{1,0:T(8,128)(2,1)S(1)} %pad_maximum_fusion.near_ref), channel_id=1, source_target_pairs={{0,1},{1,0},{2,3},{3,2},{4,5},{5,4},{6,7},{7,6},{8,9},{9,8},{10,11... | collective-permute-start | bytes 3145736 | tf_op jit(solution)/shard_map/ppermute | solution.py:79
  67.3 20.8 %all-to-all-start.2 = ((f32[8,16,192]{2,1,0:T(8,128)}), f32[8,16,192]{2,1,0:T(8,128)S(1)}, u32[]{:S(2)}, u32[]{:S(2)}) async-start(f32[8,16,192]{2,1,0:T(8,128)} %broadcast_in_dim.136), calls=%async_computation.2 | async-start | bytes 262144 | tf_op jit(solution)/shard_map/all_to_all | solution.py:83
  88.1 7.0 %copy-start.1 = (bf16[192,256]{1,0:T(8,128)(2,1)S(1)}, bf16[192,256]{1,0:T(8,128)(2,1)}, u32[]{:S(2)}) copy-start(bf16[192,256]{1,0:T(8,128)(2,1)} %param.7) | copy-start | bytes 294916
  88.1 7.1 %copy-start.2 = (bf16[192,256]{1,0:T(8,128)(2,1)S(1)}, bf16[192,256]{1,0:T(8,128)(2,1)}, u32[]{:S(2)}) copy-start(bf16[192,256]{1,0:T(8,128)(2,1)} %param.13) | copy-start | bytes 294916
  88.1 28.2 %all-to-all-start.3 = ((bf16[8,96,1024]{2,1,0:T(8,128)(2,1)}), bf16[8,96,1024]{2,1,0:T(8,128)(2,1)S(1)}, u32[]{:S(2)}, u32[]{:S(2)}) async-start(bf16[8,96,1024]{2,1,0:T(8,128)(2,1)} %bitcast.17), calls=%async_computation.3 | async-start | bytes 3145728 | tf_op jit(solution)/shard_map/all_to_all | solution.py:83
  91.9 3.1 %collective-permute-start.8 = (bf16[112,256]{1,0:T(8,128)(2,1)S(1)}, bf16[112,256]{1,0:T(8,128)(2,1)S(1)}, u32[]{:S(2)}, u32[]{:S(2)}) collective-permute-start(bf16[112,256]{1,0:T(8,128)(2,1)S(1)} %fusion.11), channel_id=1, source_target_pairs={{0,1},{1,0},{2,3},{3,2},{4,5},{5,4},{6,7},{7,6},{8,9},{9,8},{10,11... | collective-permute-start | bytes 172040 | tf_op jit(solution)/shard_map/ppermute | solution.py:79
  95.5 8.3 %collective-permute-start.9 = (bf16[192,256]{1,0:T(8,128)(2,1)S(1)}, bf16[192,256]{1,0:T(8,128)(2,1)S(1)}, u32[]{:S(2)}, u32[]{:S(2)}) collective-permute-start(bf16[192,256]{1,0:T(8,128)(2,1)S(1)} %bitcast.56), channel_id=1, source_target_pairs={{0,256},{1,257},{2,258},{3,259},{4,260},{5,261},{6,262},{7,263},{8... | collective-permute-start | bytes 294920 | tf_op jit(solution)/shard_map/ppermute | solution.py:79
  118.2 12.8 %collective-permute-start.10 = (bf16[96,512]{1,0:T(8,128)(2,1)S(1)}, bf16[96,512]{1,0:T(8,128)(2,1)S(1)}, u32[]{:S(2)}, u32[]{:S(2)}) collective-permute-start(bf16[96,512]{1,0:T(8,128)(2,1)S(1)} %get-tuple-element.31), channel_id=1, source_target_pairs={{0,0},{1,1},{2,16},{3,3},{4,32},{5,5},{6,48},{7,7},{8,64},{9,9},{1... | collective-permute-start | bytes 294920 | tf_op jit(solution)/shard_map/ppermute | solution.py:79
  121.0 11.7 %collective-permute-start.11 = (bf16[96,512]{1,0:T(8,128)(2,1)S(1)}, bf16[96,512]{1,0:T(8,128)(2,1)S(1)}, u32[]{:S(2)}, u32[]{:S(2)}) collective-permute-start(bf16[96,512]{1,0:T(8,128)(2,1)S(1)} %get-tuple-element.32), channel_id=1, source_target_pairs={{0,16},{1,3},{2,0},{3,1},{4,48},{5,7},{6,32},{7,5},{8,80},{9,11},{... | collective-permute-start | bytes 294920 | tf_op jit(solution)/shard_map/ppermute | solution.py:79
  122.9 20.7 %all-to-all-start.4 = ((bf16[8,128,256]{2,1,0:T(8,128)(2,1)}), bf16[8,128,256]{2,1,0:T(8,128)(2,1)S(1)}, u32[]{:S(2)}, u32[]{:S(2)}) async-start(bf16[8,128,256]{2,1,0:T(8,128)(2,1)} %reshape.200), calls=%async_computation.4 | async-start | bytes 1048576 | tf_op jit(solution)/shard_map/all_to_all | solution.py:83
  132.8 3.2 %collective-permute-start.12 = (bf16[192,256]{1,0:T(8,128)(2,1)S(1)}, bf16[192,256]{1,0:T(8,128)(2,1)S(1)}, u32[]{:S(2)}, u32[]{:S(2)}) collective-permute-start(bf16[192,256]{1,0:T(8,128)(2,1)S(1)} %pad_maximum_fusion.4), channel_id=1, source_target_pairs={{0,1},{1,0},{2,3},{3,2},{4,5},{5,4},{6,7},{7,6},{8,9},{9,8},{10,11... | collective-permute-start | bytes 294920 | tf_op jit(solution)/shard_map/ppermute | solution.py:79

commit v5 on v4

--- a/solution.py
+++ b/solution.py
@@ -190,9 +190,11 @@
     near, sums = together((near, sums))
     far = permute(near, SWAP_CORE)
     gathered, sums = together((gathered, sums))
-    rank_sums = jnp.sum(exchange(jnp.broadcast_to(sums[None], (RING,) + sums.shape), GROUPS_Z), 0)
+    sums = sums.astype(BF16)
+    rank_sums = exchange(jnp.broadcast_to(sums[None], (RING,) + sums.shape), GROUPS_Z)
     partial_value = product(c.reshape(1), gathered.reshape(RING * half, 4 * width), near, far)
     partial_value, rank_sums = together((partial_value, rank_sums))
+    rank_sums = jnp.sum(rank_sums.astype(F32), 0)
     spread = exchange(partial_value.reshape(RING, half, 4 * width), GROUPS_SCATTER)
     total = jnp.sum(spread.astype(F32), 0).astype(BF16)
 

time: 146 us -> 145 us (level)
  no operation moved by 1% of the time
where the time goes in v5:
time: 145 us; the launch traced here: 144 us
  starting transfers between devices  80.8 us (56%)
  waiting for transfers between devices  39.4 us (27%)
  local copies, waits for them, and re-layouts  10.5 us (7%)
  other arithmetic  5.1 us (4%)
  Pallas kernels  4.55 us (3%)
  matrix products  2.61 us (2%)
    ppermute x13, starting transfers between devices, permute(): return lax.ppermute(value, AXES, where)  45.5 us
    all_to_all x5, starting transfers between devices, exchange(): lax.all_to_all(value, AXES, 0, 0, axis_index_groups=groups, tiled=True)  35.3 us
    all_to_all x5, waiting for transfers between devices, exchange(): lax.all_to_all(value, AXES, 0, 0, axis_index_groups=groups, tiled=True)  27.8 us
    ppermute x13, waiting for transfers between devices, permute(): return lax.ppermute(value, AXES, where)  11.6 us
    pallas_call x1, Pallas kernels, product(): pl.pallas_call(product_kernel, grid=(count // tile,), in_specs=[pl.BlockS...  4.55 us
  transfers between devices with their start and end apart: 18, of which 11 were waited for; matrix products, arithmetic and copies ran while one was open for 10% of the time, Pallas kernels for 3%

profile of v5, /device:TPU:6, one launch (start us, length us, event | category | flops | bytes accessed | tf_op | source)
XLA Modules:
  0.0 144.2 jit_solution(7267564920436404651)
XLA Ops:
  1.7 1.9 %collective-permute-start = (bf16[256,256]{1,0:T(8,128)(2,1)S(1)}, bf16[256,256]{1,0:T(8,128)(2,1)S(1)}, u32[]{:S(2)}, u32[]{:S(2)}) collective-permute-start(bf16[256,256]{1,0:T(8,128)(2,1)S(1)} %get-tuple-element.41), channel_id=1, source_target_pairs={{0,1},{1,0},{2,3},{3,2},{4,5},{5,4},{6,7},{7,6},{8,9},{9,8},{10,11... | collective-permute-start | bytes 393224 | tf_op jit(solution)/shard_map/ppermute | solution.py:79
  5.2 2.7 %collective-permute-start.4 = (bf16[96,512]{1,0:T(8,128)(2,1)S(1)}, bf16[96,512]{1,0:T(8,128)(2,1)S(1)}, u32[]{:S(2)}, u32[]{:S(2)}) collective-permute-start(bf16[96,512]{1,0:T(8,128)(2,1)S(1)} %get-tuple-element.49), channel_id=1, source_target_pairs={{0,2},{1,3},{2,0},{3,35},{4,6},{5,67},{6,4},{7,99},{8,10},{9,131},... | collective-permute-start | bytes 294920 | tf_op jit(solution)/shard_map/ppermute | solution.py:79
  8.0 3.1 %collective-permute-start.2 = (bf16[256,512]{1,0:T(8,128)(2,1)S(1)}, bf16[256,512]{1,0:T(8,128)(2,1)S(1)}, u32[]{:S(2)}, u32[]{:S(2)}) collective-permute-start(bf16[256,512]{1,0:T(8,128)(2,1)S(1)} %copy-done), channel_id=1, source_target_pairs={{0,2},{1,3},{2,0},{3,1},{4,6},{5,7},{6,4},{7,5},{8,10},{9,11},{10,... | collective-permute-start | bytes 786440 | tf_op jit(solution)/shard_map/ppermute | solution.py:79
  12.6 7.1 %all-to-all-start = ((bf16[8,64,512]{2,1,0:T(8,128)(2,1)}), bf16[8,64,512]{2,1,0:T(8,128)(2,1)S(1)}, u32[]{:S(2)}, u32[]{:S(2)}) async-start(bf16[8,64,512]{2,1,0:T(8,128)(2,1)} %broadcast_in_dim.124), calls=%async_computation | async-start | bytes 1048576 | tf_op jit(solution)/shard_map/all_to_all | solution.py:83
  20.0 5.3 %collective-permute-start.3 = (bf16[520,512]{1,0:T(8,128)(2,1)S(1)}, bf16[520,512]{1,0:T(8,128)(2,1)}, u32[]{:S(2)}, u32[]{:S(2)}) collective-permute-start(bf16[520,512]{1,0:T(8,128)(2,1)S(1)} %maximum_maximum_fusion), channel_id=1, source_target_pairs={{0,256},{1,257},{2,258},{3,259},{4,260},{5,261},{6,262},{7,263},{8... | collective-permute-start | bytes 1597448 | tf_op jit(solution)/shard_map/ppermute | solution.py:79
  25.4 7.0 %all-to-all-done = bf16[8,64,512]{2,1,0:T(8,128)(2,1)S(1)} async-done(((bf16[8,64,512]{2,1,0:T(8,128)(2,1)}), bf16[8,64,512]{2,1,0:T(8,128)(2,1)S(1)}, u32[]{:S(2)}, u32[]{:S(2)}) %all-to-all-start) | async-done | bytes 524320 | tf_op jit(solution)/shard_map/all_to_all | solution.py:83
  33.8 4.7 %all-to-all-start.1 = ((bf16[8,96,1024]{2,1,0:T(8,128)(2,1)}), bf16[8,96,1024]{2,1,0:T(8,128)(2,1)S(1)}, u32[]{:S(2)}, u32[]{:S(2)}) async-start(bf16[8,96,1024]{2,1,0:T(8,128)(2,1)} %broadcast_in_dim.125), calls=%async_computation.1 | async-start | bytes 3145728 | tf_op jit(solution)/shard_map/all_to_all | solution.py:83
  40.2 3.6 %collective-permute-start.5 = (bf16[96,512]{1,0:T(8,128)(2,1)S(1)}, bf16[96,512]{1,0:T(8,128)(2,1)S(1)}, u32[]{:S(2)}, u32[]{:S(2)}) collective-permute-start(bf16[96,512]{1,0:T(8,128)(2,1)S(1)} %bitcast_select_fusion.2), channel_id=1, source_target_pairs={{0,256},{1,257},{2,258},{3,259},{4,260},{5,261},{6,262},{7,263},{8... | collective-permute-start | bytes 294920 | tf_op jit(solution)/shard_map/ppermute | solution.py:79
  44.0 1.9 %slice.106 = bf16[512,512]{1,0:T(8,128)(2,1)} slice(bf16[520,512]{1,0:T(8,128)(2,1)} %collective-permute-done.3), slice={[0:512], [0:512]} | slice | bytes 1048576 | tf_op jit(solution)/shard_map/slice | solution.py:171
  48.5 6.4 %collective-permute-start.6 = (f32[16,192]{1,0:T(8,128)S(1)}, f32[16,192]{1,0:T(8,128)S(1)}, u32[]{:S(2)}, u32[]{:S(2)}) collective-permute-start(f32[16,192]{1,0:T(8,128)S(1)} %fusion.1), channel_id=1, source_target_pairs={{0,2},{1,3},{2,0},{3,1},{4,6},{5,7},{6,4},{7,5},{8,10},{9,11},{10,... | collective-permute-start | bytes 36872 | tf_op jit(solution)/shard_map/ppermute | solution.py:79
  56.6 10.0 %collective-permute-start.7 = (bf16[512,1024]{1,0:T(8,128)(2,1)S(1)}, bf16[512,1024]{1,0:T(8,128)(2,1)}, u32[]{:S(2)}, u32[]{:S(2)}) collective-permute-start(bf16[512,1024]{1,0:T(8,128)(2,1)S(1)} %pad_maximum_fusion.near_ref), channel_id=1, source_target_pairs={{0,1},{1,0},{2,3},{3,2},{4,5},{5,4},{6,7},{7,6},{8,9},{9,8},{10,11... | collective-permute-start | bytes 3145736 | tf_op jit(solution)/shard_map/ppermute | solution.py:79
  67.2 11.7 %all-to-all-start.2 = ((bf16[8,16,192]{2,1,0:T(8,128)(2,1)}), bf16[8,16,192]{2,1,0:T(8,128)(2,1)S(1)}, u32[]{:S(2)}, u32[]{:S(2)}) async-start(bf16[8,16,192]{2,1,0:T(8,128)(2,1)} %broadcast_in_dim.136), calls=%async_computation.2 | async-start | bytes 131072 | tf_op jit(solution)/shard_map/all_to_all | solution.py:83
  79.0 4.6 %shard_map.102 = bf16[768,1024]{1,0:T(8,128)(2,1)} custom-call(s32[1]{0:T(128)} %bitcast.5.core_ref, bf16[768,1024]{1,0:T(8,128)(2,1)S(1)} %bitcast.43, bf16[512,1024]{1,0:T(8,128)(2,1)S(1)} %pad_maximum_fusion.near_ref, bf16[512,1024]{1,0:T(8,128)(2,1)} %collective-permute-done.7.far_ref), custom_call_target="tpu_custom_call" | custom-call | flops 1610612736 | bytes 5242880 | tf_op jit(solution)/shard_map/pallas_call | solution.py:112
  83.5 3.8 %all-to-all-done.2 = bf16[8,16,192]{2,1,0:T(8,128)(2,1)S(1)} async-done(((bf16[8,16,192]{2,1,0:T(8,128)(2,1)}), bf16[8,16,192]{2,1,0:T(8,128)(2,1)S(1)}, u32[]{:S(2)}, u32[]{:S(2)}) %all-to-all-start.2) | async-done | bytes 49184 | tf_op jit(solution)/shard_map/all_to_all | solution.py:83
  87.4 3.7 %all-to-all-start.3 = ((bf16[8,96,1024]{2,1,0:T(8,128)(2,1)}), bf16[8,96,1024]{2,1,0:T(8,128)(2,1)S(1)}, u32[]{:S(2)}, u32[]{:S(2)}) async-start(bf16[8,96,1024]{2,1,0:T(8,128)(2,1)} %bitcast.17), calls=%async_computation.3 | async-start | bytes 3145728 | tf_op jit(solution)/shard_map/all_to_all | solution.py:83
  91.2 1.9 %collective-permute-start.8 = (bf16[112,256]{1,0:T(8,128)(2,1)S(1)}, bf16[112,256]{1,0:T(8,128)(2,1)S(1)}, u32[]{:S(2)}, u32[]{:S(2)}) collective-permute-start(bf16[112,256]{1,0:T(8,128)(2,1)S(1)} %fusion.11), channel_id=1, source_target_pairs={{0,1},{1,0},{2,3},{3,2},{4,5},{5,4},{6,7},{7,6},{8,9},{9,8},{10,11... | collective-permute-start | bytes 172040 | tf_op jit(solution)/shard_map/ppermute | solution.py:79
  94.7 3.3 %collective-permute-start.9 = (bf16[192,256]{1,0:T(8,128)(2,1)S(1)}, bf16[192,256]{1,0:T(8,128)(2,1)S(1)}, u32[]{:S(2)}, u32[]{:S(2)}) collective-permute-start(bf16[192,256]{1,0:T(8,128)(2,1)S(1)} %bitcast.56), channel_id=1, source_target_pairs={{0,256},{1,257},{2,258},{3,259},{4,260},{5,261},{6,262},{7,263},{8... | collective-permute-start | bytes 294920 | tf_op jit(solution)/shard_map/ppermute | solution.py:79
  98.3 4.7 %collective-permute-done.9 = bf16[192,256]{1,0:T(8,128)(2,1)S(1)} collective-permute-done((bf16[192,256]{1,0:T(8,128)(2,1)S(1)}, bf16[192,256]{1,0:T(8,128)(2,1)S(1)}, u32[]{:S(2)}, u32[]{:S(2)}) %collective-permute-start.9) | collective-permute-done | bytes 98336 | tf_op jit(solution)/shard_map/ppermute | solution.py:79
  105.2 10.3 %all-to-all-done.3 = bf16[8,96,1024]{2,1,0:T(8,128)(2,1)S(1)} async-done(((bf16[8,96,1024]{2,1,0:T(8,128)(2,1)}), bf16[8,96,1024]{2,1,0:T(8,128)(2,1)S(1)}, u32[]{:S(2)}, u32[]{:S(2)}) %all-to-all-start.3) | async-done | bytes 1572896 | tf_op jit(solution)/shard_map/all_to_all | solution.py:83
  117.5 2.8 %collective-permute-start.10 = (bf16[96,512]{1,0:T(8,128)(2,1)S(1)}, bf16[96,512]{1,0:T(8,128)(2,1)S(1)}, u32[]{:S(2)}, u32[]{:S(2)}) collective-permute-start(bf16[96,512]{1,0:T(8,128)(2,1)S(1)} %get-tuple-element.31), channel_id=1, source_target_pairs={{0,0},{1,1},{2,16},{3,3},{4,32},{5,5},{6,48},{7,7},{8,64},{9,9},{1... | collective-permute-start | bytes 294920 | tf_op jit(solution)/shard_map/ppermute | solution.py:79
  120.2 1.9 %collective-permute-start.11 = (bf16[96,512]{1,0:T(8,128)(2,1)S(1)}, bf16[96,512]{1,0:T(8,128)(2,1)S(1)}, u32[]{:S(2)}, u32[]{:S(2)}) collective-permute-start(bf16[96,512]{1,0:T(8,128)(2,1)S(1)} %get-tuple-element.32), channel_id=1, source_target_pairs={{0,16},{1,3},{2,0},{3,1},{4,48},{5,7},{6,32},{7,5},{8,80},{9,11},{... | collective-permute-start | bytes 294920 | tf_op jit(solution)/shard_map/ppermute | solution.py:79
  122.2 8.1 %all-to-all-start.4 = ((bf16[8,128,256]{2,1,0:T(8,128)(2,1)}), bf16[8,128,256]{2,1,0:T(8,128)(2,1)S(1)}, u32[]{:S(2)}, u32[]{:S(2)}) async-start(bf16[8,128,256]{2,1,0:T(8,128)(2,1)} %reshape.200), calls=%async_computation.4 | async-start | bytes 1048576 | tf_op jit(solution)/shard_map/all_to_all | solution.py:83
  132.0 1.9 %collective-permute-start.12 = (bf16[192,256]{1,0:T(8,128)(2,1)S(1)}, bf16[192,256]{1,0:T(8,128)(2,1)S(1)}, u32[]{:S(2)}, u32[]{:S(2)}) collective-permute-start(bf16[192,256]{1,0:T(8,128)(2,1)S(1)} %pad_maximum_fusion.4), channel_id=1, source_target_pairs={{0,1},{1,0},{2,3},{3,2},{4,5},{5,4},{6,7},{7,6},{8,9},{9,8},{10,11... | collective-permute-start | bytes 294920 | tf_op jit(solution)/shard_map/ppermute | solution.py:79
  136.9 6.6 %all-to-all-done.4 = bf16[8,128,256]{2,1,0:T(8,128)(2,1)S(1)} async-done(((bf16[8,128,256]{2,1,0:T(8,128)(2,1)}), bf16[8,128,256]{2,1,0:T(8,128)(2,1)S(1)}, u32[]{:S(2)}, u32[]{:S(2)}) %all-to-all-start.4) | async-done | bytes 524320 | tf_op jit(solution)/shard_map/all_to_all | solution.py:83
  (88 shorter events, 24.0 us)
Async XLA Ops:
  0.6 7.3 %copy-start = (bf16[256,512]{1,0:T(8,128)(2,1)S(1)}, bf16[256,512]{1,0:T(8,128)(2,1)}, u32[]{:S(2)}) copy-start(bf16[256,512]{1,0:T(8,128)(2,1)} %param.8) | copy-start | bytes 786436
  1.7 3.2 %collective-permute-start = (bf16[256,256]{1,0:T(8,128)(2,1)S(1)}, bf16[256,256]{1,0:T(8,128)(2,1)S(1)}, u32[]{:S(2)}, u32[]{:S(2)}) collective-permute-start(bf16[256,256]{1,0:T(8,128)(2,1)S(1)} %get-tuple-element.41), channel_id=1, source_target_pairs={{0,1},{1,0},{2,3},{3,2},{4,5},{5,4},{6,7},{7,6},{8,9},{9,8},{10,11... | collective-permute-start | bytes 393224 | tf_op jit(solution)/shard_map/ppermute | solution.py:79
  5.0 14.8 %copy-start.3 = (s32[1,6]{1,0:T(1,128)S(1)}, s32[1,6]{1,0:T(1,128)}, u32[]{:S(2)}) copy-start(s32[1,6]{1,0:T(1,128)} %param.11) | copy-start | bytes 76
  5.2 14.5 %collective-permute-start.4 = (bf16[96,512]{1,0:T(8,128)(2,1)S(1)}, bf16[96,512]{1,0:T(8,128)(2,1)S(1)}, u32[]{:S(2)}, u32[]{:S(2)}) collective-permute-start(bf16[96,512]{1,0:T(8,128)(2,1)S(1)} %get-tuple-element.49), channel_id=1, source_target_pairs={{0,2},{1,3},{2,0},{3,35},{4,6},{5,67},{6,4},{7,99},{8,10},{9,131},... | collective-permute-start | bytes 294920 | tf_op jit(solution)/shard_map/ppermute | solution.py:79
  8.0 11.8 %collective-permute-start.2 = (bf16[256,512]{1,0:T(8,128)(2,1)S(1)}, bf16[256,512]{1,0:T(8,128)(2,1)S(1)}, u32[]{:S(2)}, u32[]{:S(2)}) collective-permute-start(bf16[256,512]{1,0:T(8,128)(2,1)S(1)} %copy-done), channel_id=1, source_target_pairs={{0,2},{1,3},{2,0},{3,1},{4,6},{5,7},{6,4},{7,5},{8,10},{9,11},{10,... | collective-permute-start | bytes 786440 | tf_op jit(solution)/shard_map/ppermute | solution.py:79
  11.1 8.7 %collective-permute-start.1 = (bf16[96,512]{1,0:T(8,128)(2,1)S(1)}, bf16[96,512]{1,0:T(8,128)(2,1)S(1)}, u32[]{:S(2)}, u32[]{:S(2)}) collective-permute-start(bf16[96,512]{1,0:T(8,128)(2,1)S(1)} %get-tuple-element.48), channel_id=1, source_target_pairs={{0,0},{1,1},{2,2},{3,33},{4,4},{5,65},{6,6},{7,97},{8,8},{9,129},{... | collective-permute-start | bytes 294920 | tf_op jit(solution)/shard_map/ppermute | solution.py:79
  12.6 19.8 %all-to-all-start = ((bf16[8,64,512]{2,1,0:T(8,128)(2,1)}), bf16[8,64,512]{2,1,0:T(8,128)(2,1)S(1)}, u32[]{:S(2)}, u32[]{:S(2)}) async-start(bf16[8,64,512]{2,1,0:T(8,128)(2,1)} %broadcast_in_dim.124), calls=%async_computation | async-start | bytes 1048576 | tf_op jit(solution)/shard_map/all_to_all | solution.py:83
  20.0 18.5 %collective-permute-start.3 = (bf16[520,512]{1,0:T(8,128)(2,1)S(1)}, bf16[520,512]{1,0:T(8,128)(2,1)}, u32[]{:S(2)}, u32[]{:S(2)}) collective-permute-start(bf16[520,512]{1,0:T(8,128)(2,1)S(1)} %maximum_maximum_fusion), channel_id=1, source_target_pairs={{0,256},{1,257},{2,258},{3,259},{4,260},{5,261},{6,262},{7,263},{8... | collective-permute-start | bytes 1597448 | tf_op jit(solution)/shard_map/ppermute | solution.py:79
  33.8 32.8 %all-to-all-start.1 = ((bf16[8,96,1024]{2,1,0:T(8,128)(2,1)}), bf16[8,96,1024]{2,1,0:T(8,128)(2,1)S(1)}, u32[]{:S(2)}, u32[]{:S(2)}) async-start(bf16[8,96,1024]{2,1,0:T(8,128)(2,1)} %broadcast_in_dim.125), calls=%async_computation.1 | async-start | bytes 3145728 | tf_op jit(solution)/shard_map/all_to_all | solution.py:83
  40.2 8.0 %collective-permute-start.5 = (bf16[96,512]{1,0:T(8,128)(2,1)S(1)}, bf16[96,512]{1,0:T(8,128)(2,1)S(1)}, u32[]{:S(2)}, u32[]{:S(2)}) collective-permute-start(bf16[96,512]{1,0:T(8,128)(2,1)S(1)} %bitcast_select_fusion.2), channel_id=1, source_target_pairs={{0,256},{1,257},{2,258},{3,259},{4,260},{5,261},{6,262},{7,263},{8... | collective-permute-start | bytes 294920 | tf_op jit(solution)/shard_map/ppermute | solution.py:79
  48.5 8.1 %collective-permute-start.6 = (f32[16,192]{1,0:T(8,128)S(1)}, f32[16,192]{1,0:T(8,128)S(1)}, u32[]{:S(2)}, u32[]{:S(2)}) collective-permute-start(f32[16,192]{1,0:T(8,128)S(1)} %fusion.1), channel_id=1, source_target_pairs={{0,2},{1,3},{2,0},{3,1},{4,6},{5,7},{6,4},{7,5},{8,10},{9,11},{10,... | collective-permute-start | bytes 36872 | tf_op jit(solution)/shard_map/ppermute | solution.py:79
  56.6 22.4 %collective-permute-start.7 = (bf16[512,1024]{1,0:T(8,128)(2,1)S(1)}, bf16[512,1024]{1,0:T(8,128)(2,1)}, u32[]{:S(2)}, u32[]{:S(2)}) collective-permute-start(bf16[512,1024]{1,0:T(8,128)(2,1)S(1)} %pad_maximum_fusion.near_ref), channel_id=1, source_target_pairs={{0,1},{1,0},{2,3},{3,2},{4,5},{5,4},{6,7},{7,6},{8,9},{9,8},{10,11... | collective-permute-start | bytes 3145736 | tf_op jit(solution)/shard_map/ppermute | solution.py:79
  67.2 20.1 %all-to-all-start.2 = ((bf16[8,16,192]{2,1,0:T(8,128)(2,1)}), bf16[8,16,192]{2,1,0:T(8,128)(2,1)S(1)}, u32[]{:S(2)}, u32[]{:S(2)}) async-start(bf16[8,16,192]{2,1,0:T(8,128)(2,1)} %broadcast_in_dim.136), calls=%async_computation.2 | async-start | bytes 131072 | tf_op jit(solution)/shard_map/all_to_all | solution.py:83
  87.4 7.0 %copy-start.1 = (bf16[192,256]{1,0:T(8,128)(2,1)S(1)}, bf16[192,256]{1,0:T(8,128)(2,1)}, u32[]{:S(2)}) copy-start(bf16[192,256]{1,0:T(8,128)(2,1)} %param.7) | copy-start | bytes 294916
  87.4 7.1 %copy-start.2 = (bf16[192,256]{1,0:T(8,128)(2,1)S(1)}, bf16[192,256]{1,0:T(8,128)(2,1)}, u32[]{:S(2)}) copy-start(bf16[192,256]{1,0:T(8,128)(2,1)} %param.13) | copy-start | bytes 294916
  87.4 28.2 %all-to-all-start.3 = ((bf16[8,96,1024]{2,1,0:T(8,128)(2,1)}), bf16[8,96,1024]{2,1,0:T(8,128)(2,1)S(1)}, u32[]{:S(2)}, u32[]{:S(2)}) async-start(bf16[8,96,1024]{2,1,0:T(8,128)(2,1)} %bitcast.17), calls=%async_computation.3 | async-start | bytes 3145728 | tf_op jit(solution)/shard_map/all_to_all | solution.py:83
  91.2 3.1 %collective-permute-start.8 = (bf16[112,256]{1,0:T(8,128)(2,1)S(1)}, bf16[112,256]{1,0:T(8,128)(2,1)S(1)}, u32[]{:S(2)}, u32[]{:S(2)}) collective-permute-start(bf16[112,256]{1,0:T(8,128)(2,1)S(1)} %fusion.11), channel_id=1, source_target_pairs={{0,1},{1,0},{2,3},{3,2},{4,5},{5,4},{6,7},{7,6},{8,9},{9,8},{10,11... | collective-permute-start | bytes 172040 | tf_op jit(solution)/shard_map/ppermute | solution.py:79
  94.7 8.3 %collective-permute-start.9 = (bf16[192,256]{1,0:T(8,128)(2,1)S(1)}, bf16[192,256]{1,0:T(8,128)(2,1)S(1)}, u32[]{:S(2)}, u32[]{:S(2)}) collective-permute-start(bf16[192,256]{1,0:T(8,128)(2,1)S(1)} %bitcast.56), channel_id=1, source_target_pairs={{0,256},{1,257},{2,258},{3,259},{4,260},{5,261},{6,262},{7,263},{8... | collective-permute-start | bytes 294920 | tf_op jit(solution)/shard_map/ppermute | solution.py:79
  117.5 12.8 %collective-permute-start.10 = (bf16[96,512]{1,0:T(8,128)(2,1)S(1)}, bf16[96,512]{1,0:T(8,128)(2,1)S(1)}, u32[]{:S(2)}, u32[]{:S(2)}) collective-permute-start(bf16[96,512]{1,0:T(8,128)(2,1)S(1)} %get-tuple-element.31), channel_id=1, source_target_pairs={{0,0},{1,1},{2,16},{3,3},{4,32},{5,5},{6,48},{7,7},{8,64},{9,9},{1... | collective-permute-start | bytes 294920 | tf_op jit(solution)/shard_map/ppermute | solution.py:79
  120.2 11.7 %collective-permute-start.11 = (bf16[96,512]{1,0:T(8,128)(2,1)S(1)}, bf16[96,512]{1,0:T(8,128)(2,1)S(1)}, u32[]{:S(2)}, u32[]{:S(2)}) collective-permute-start(bf16[96,512]{1,0:T(8,128)(2,1)S(1)} %get-tuple-element.32), channel_id=1, source_target_pairs={{0,16},{1,3},{2,0},{3,1},{4,48},{5,7},{6,32},{7,5},{8,80},{9,11},{... | collective-permute-start | bytes 294920 | tf_op jit(solution)/shard_map/ppermute | solution.py:79
  122.2 21.4 %all-to-all-start.4 = ((bf16[8,128,256]{2,1,0:T(8,128)(2,1)}), bf16[8,128,256]{2,1,0:T(8,128)(2,1)S(1)}, u32[]{:S(2)}, u32[]{:S(2)}) async-start(bf16[8,128,256]{2,1,0:T(8,128)(2,1)} %reshape.200), calls=%async_computation.4 | async-start | bytes 1048576 | tf_op jit(solution)/shard_map/all_to_all | solution.py:83
  132.0 3.2 %collective-permute-start.12 = (bf16[192,256]{1,0:T(8,128)(2,1)S(1)}, bf16[192,256]{1,0:T(8,128)(2,1)S(1)}, u32[]{:S(2)}, u32[]{:S(2)}) collective-permute-start(bf16[192,256]{1,0:T(8,128)(2,1)S(1)} %pad_maximum_fusion.4), channel_id=1, source_target_pairs={{0,1},{1,0},{2,3},{3,2},{4,5},{5,4},{6,7},{7,6},{8,9},{9,8},{10,11... | collective-permute-start | bytes 294920 | tf_op jit(solution)/shard_map/ppermute | solution.py:79
